TPU v7x, 128 devices: a whole 4x4x4 slice. The times are simulated.
128 devices in a mesh: ctx: 32 (over y_hi, z, x), head: 4 (over y_lo, core).
Axes of the slice: x: 4, y: 4 (y_hi: 2, y_lo: 2; y = y_hi * 2 + y_lo), z: 4, core: 2. Of those that a mesh axis runs over, the one named last changes fastest.
Arguments:
- queries: bfloat16 [8192, 32, 128], P('ctx', 'head'), may hold values from -40 to 40
- key_rows: bfloat16 [8192, 4, 128], P('ctx', 'head'), may hold values from -4 to 4
- value_matrix: bfloat16 [8192, 4, 128], P('ctx', 'head'), may hold values from -6 to 6
- out_weight: bfloat16 [4096, 5120], P('head'), may hold values from -0.09375 to 0.09375
- cotangent: bfloat16 [8192, 5120], P(('ctx', 'head')), may hold values from -6 to 6
Outputs:
- output: bfloat16 [8192, 5120], P(('ctx', 'head'))
- grad_queries: bfloat16 [8192, 32, 128], P('ctx', 'head')
- grad_keys: bfloat16 [8192, 4, 128], P('ctx', 'head')
- grad_values: bfloat16 [8192, 4, 128], P('ctx', 'head')
All inputs are finite; a program needn't handle non-finite values.
Results may differ from a plain program's by a relative error of at most 0.039.
Values may be sent and summed in bfloat16 or wider, within the bound.
A program may use at most 128 MiB of HBM per device.

v0:
```python
import math

import jax
import jax.numpy as jnp
from jax import lax
from jax.sharding import PartitionSpec as P


def tile_scores(query_collection, query_pos, block_keys, key_start, scale):
    scores = (
        jnp.einsum(
            "twcp,swp->wcts", query_collection, block_keys, preferred_element_type=jnp.float32
        )
        * scale
    )
    key_pos = key_start + jnp.arange(block_keys.shape[0], dtype=jnp.int32)
    return jnp.where(key_pos[None, :] <= query_pos[:, None], scores, -jnp.inf)


def attend_forward(query_collection, query_pos, key_all, value_all, scale, block):
    limit = jnp.max(query_pos) // block + 1
    stat_shape = (query_collection.shape[1], query_collection.shape[2], query_collection.shape[0])

    def first_pass(index, carry):
        top, total = carry
        start = index * block
        block_keys = lax.dynamic_slice_in_dim(key_all, start, block, 0)
        scores = tile_scores(query_collection, query_pos, block_keys, start, scale)
        new_top = jnp.maximum(top, jnp.max(scores, axis=-1))
        total = total * jnp.exp(top - new_top) + jnp.sum(
            jnp.exp(scores - new_top[..., None]), axis=-1
        )
        return (new_top, total)

    start_stats = (jnp.full(stat_shape, -jnp.inf, jnp.float32), jnp.zeros(stat_shape, jnp.float32))
    top, total = lax.fori_loop(0, limit, first_pass, start_stats)
    lse = top + jnp.log(total)

    def second_pass(index, summed):
        start = index * block
        block_keys = lax.dynamic_slice_in_dim(key_all, start, block, 0)
        block_values = lax.dynamic_slice_in_dim(value_all, start, block, 0)
        scores = tile_scores(query_collection, query_pos, block_keys, start, scale)
        weight_tensors = jnp.exp(scores - lse[..., None]).astype(jnp.bfloat16)
        return summed + jnp.einsum(
            "hmyi,iht->yhmt", weight_tensors, block_values, preferred_element_type=jnp.float32
        )

    summed = lax.fori_loop(0, limit, second_pass, jnp.zeros(query_collection.shape, jnp.float32))
    return (summed.astype(jnp.bfloat16), lse)


def tile_grads(
    query_collection, gradient_group, lse, delta, query_pos, block_keys, block_values, start, scale
):
    scores = tile_scores(query_collection, query_pos, block_keys, start, scale)
    probs = jnp.exp(scores - lse[..., None])
    grad_weights = jnp.einsum(
        "twcp,swp->wcts", gradient_group, block_values, preferred_element_type=jnp.float32
    )
    score_gradient = (probs * (grad_weights - delta[..., None]) * scale).astype(jnp.bfloat16)
    return (probs.astype(jnp.bfloat16), score_gradient)


def backward_joint(
    query_collection,
    gradient_group,
    lse,
    delta,
    query_pos,
    key_all,
    value_all,
    scale,
    block,
    key_sum,
):
    limit = jnp.max(query_pos) // block + 1

    def step(index, carry):
        grad_query, key_sum = carry
        start = index * block
        block_keys = lax.dynamic_slice_in_dim(key_all, start, block, 0)
        block_values = lax.dynamic_slice_in_dim(value_all, start, block, 0)
        weight_tensors, score_gradient = tile_grads(
            query_collection,
            gradient_group,
            lse,
            delta,
            query_pos,
            block_keys,
            block_values,
            start,
            scale,
        )
        grad_query = grad_query + jnp.einsum(
            "hmyi,iht->yhmt", score_gradient, block_keys, preferred_element_type=jnp.float32
        )
        key_part = jnp.einsum(
            "jqzo,zjqy->ojy", score_gradient, query_collection, preferred_element_type=jnp.float32
        )
        value_part = jnp.einsum(
            "jqzo,zjqy->ojy", weight_tensors, gradient_group, preferred_element_type=jnp.float32
        )
        previous = lax.dynamic_slice_in_dim(key_sum, start, block, 0)
        key_sum = lax.dynamic_update_slice_in_dim(
            key_sum, previous + jnp.stack([key_part, value_part], 1), start, 0
        )
        return (grad_query, key_sum)

    return lax.fori_loop(0, limit, step, (jnp.zeros(query_collection.shape, jnp.float32), key_sum))


def local(queries, key_rows, value_matrix, out_weight, cotangent):
    rows, local_heads, head_dim = queries.shape
    kv_local = key_rows.shape[1]
    group = local_heads // kv_local
    scale = 1.0 / math.sqrt(head_dim)
    position = lax.axis_index("ctx")
    key_all, value_all = (
        lax.all_gather(key_rows, "ctx", axis=0, tiled=True),
        lax.all_gather(value_matrix, "ctx", axis=0, tiled=True),
    )
    block = min(512, key_all.shape[0])
    query_grouped = queries.reshape(rows, kv_local, group, head_dim)
    query_sets = [query_grouped]
    positions = [position * rows + jnp.arange(rows, dtype=jnp.int32)]
    results = [
        attend_forward(query_collection, query_pos, key_all, value_all, scale, block)
        for query_collection, query_pos in zip(query_sets, positions)
    ]
    attn_sets = [result[0] for result in results]
    lse_sets = [result[1] for result in results]
    attn_home = attn_sets[0]
    attn_flat = attn_home.reshape(rows, local_heads * head_dim)
    output = lax.psum_scatter(
        jnp.dot(attn_flat, out_weight, preferred_element_type=jnp.float32),
        "head",
        scatter_dimension=0,
        tiled=True,
    ).astype(jnp.bfloat16)
    product = lax.dot_general(
        lax.all_gather(cotangent, "head", axis=0, tiled=True),
        out_weight,
        (((1,), (1,)), ((), ())),
        preferred_element_type=jnp.float32,
    )
    grad_attn = product.astype(jnp.bfloat16)
    grad_grouped = grad_attn.reshape(rows, kv_local, group, head_dim)
    grad_sets = [grad_grouped]
    delta_sets = [
        jnp.transpose(
            jnp.sum(gradient_group.astype(jnp.float32) * attn_set.astype(jnp.float32), axis=-1),
            (1, 2, 0),
        )
        for gradient_group, attn_set in zip(grad_sets, attn_sets)
    ]
    packed = list(zip(query_sets, grad_sets, lse_sets, delta_sets, positions))
    key_sum = jnp.zeros((key_all.shape[0], 2, kv_local, head_dim), jnp.float32)
    query_grads = []
    for query_collection, gradient_group, lse, delta, query_pos in packed:
        grad_query, key_sum = backward_joint(
            query_collection,
            gradient_group,
            lse,
            delta,
            query_pos,
            key_all,
            value_all,
            scale,
            block,
            key_sum,
        )
        query_grads.append(grad_query)
    key_own = lax.psum_scatter(key_sum, "ctx", scatter_dimension=0, tiled=True)
    query_low = [grad_query.astype(jnp.bfloat16) for grad_query in query_grads]
    query_home = query_low[0]
    grad_queries = query_home.reshape(rows, local_heads, head_dim)
    grad_keys = key_own[:, 0].astype(jnp.bfloat16)
    grad_values = key_own[:, 1].astype(jnp.bfloat16)
    return (output, grad_queries, grad_keys, grad_values)


def solution(mesh):
    return jax.shard_map(
        local,
        mesh=mesh,
        in_specs=(
            P("ctx", "head", None),
            P("ctx", "head", None),
            P("ctx", "head", None),
            P("head", None),
            P(("ctx", "head"), None),
        ),
        out_specs=(
            P(("ctx", "head"), None),
            P("ctx", "head", None),
            P("ctx", "head", None),
            P("ctx", "head", None),
        ),
        check_vma=False,
    )
```

profile of v0, /device:TPU:0, one launch (start us, length us, event | category | flops | bytes accessed | tf_op | source)
XLA Modules:
  0.0 602.2 jit_solution(11611865945384629272)
XLA Ops:
  7.2 0.7 all-gather.8.cloned.1.call-update
  7.9 0.7 all-gather.6.cloned.1.call-update
  8.7 0.7 all-gather.4.cloned.1.call-update
  9.4 0.6 add_reduce_fusion
  12.7 1.1 copy.24
  13.8 31.6 %all-gather.8.cloned.1.call-done = bf16[256,5120]{1,0:T(8,128)(2,1)} async-done(((bf16[64,5120]{1,0:T(8,128)(2,1)}), bf16[256,5120]{1,0:T(8,128)(2,1)}) %all-gather.8.cloned.1.call-update) | async-done | bytes 2621456 | tf_op jit(solution)/shard_map/all_gather | solution.py:142
  45.3 7.7 %fusion.78 = bf16[32,8,8,128]{3,1,2,0:T(8,128)(2,1)S(1)} fusion(bf16[256,5120]{1,0:T(8,128)(2,1)} %all-gather.8.cloned.1.call-done, bf16[1024,5120]{1,0:T(8,128)(2,1)} %param.14), kind=kOutput, calls=%fused_computation.76 | convolution fusion | flops 2684616704 | bytes 13631488 | tf_op jit(solution)/shard_map/dot_general | solution.py:141
  53.1 0.3 copy.14
  53.5 66.9 %all-gather.6.cloned.1.call-done = bf16[8192,1,128]{2,0,1:T(8,128)(2,1)} async-done(((bf16[256,1,128]{2,0,1:T(8,128)(2,1)}), bf16[8192,1,128]{2,0,1:T(8,128)(2,1)}) %all-gather.6.cloned.1.call-update) | async-done | bytes 2097168 | tf_op jit(solution)/shard_map/all_gather | solution.py:120
  120.4 2.7 while.37
  120.4 0.1 broadcast_compare_fusion.6
  120.6 1.7 fusion.106
  122.2 0.9 exponential_reduce_fusion.2
  123.2 68.0 %all-gather.4.cloned.1.call-done = bf16[8192,1,128]{2,0,1:T(8,128)(2,1)} async-done(((bf16[256,1,128]{2,0,1:T(8,128)(2,1)}), bf16[8192,1,128]{2,0,1:T(8,128)(2,1)}) %all-gather.4.cloned.1.call-update) | async-done | bytes 2097168 | tf_op jit(solution)/shard_map/all_gather | solution.py:121
  191.2 2.6 while.38
  191.4 2.4 fusion.111
  194.0 8.8 %fusion.79 = f32[256,5120]{1,0:T(8,128)} fusion(bf16[256,1024]{0,1:T(8,128)(2,1)S(1)} %bitcast.254, bf16[1024,5120]{1,0:T(8,128)(2,1)} %param.14), kind=kOutput, calls=%fused_computation.84 | convolution fusion | flops 2684354560 | bytes 16252928 | tf_op jit(solution)/shard_map/dot_general | solution.py:136
  203.0 3.8 broadcast_in_dim.41
  206.7 9.3 %while.39 = (s32[]{:T(128)}, f32[256,1,8,128]{0,3,2,1:T(8,128)S(1)}, f32[8192,2,1,128]{3,0,2,1:T(8,128)}, s32[]{:T(128)}, bf16[8192,1,128]{2,0,1:T(8,128)(2,1)},...) while((s32[]{:T(128)}, ...), condition=%wide.region_10.11_spmd.clone, body=%wide.region_9.10_spmd.clone.sunk | while | flops 1354367744 | bytes 25983188 | solution.py:110
  206.7 0.1 broadcast_compare_fusion.8
  206.9 1.6 fusion.122
  208.5 1.0 fusion.125
  209.6 2.4 fusion.123
  212.0 0.7 fusion.126
  212.7 1.4 fusion.124
  214.1 1.9 fusion.127
  216.0 1.2 copy.16
  217.2 75.0 %reduce-scatter.3.cloned.1.call-done = f32[64,5120]{1,0:T(8,128)} async-done(((f32[256,5120]{1,0:T(8,128)}), f32[64,5120]{1,0:T(8,128)}) %reduce-scatter.3.cloned.1.call-update) | async-done | bytes 1310736 | tf_op jit(solution)/shard_map/reduce_scatter | solution.py:135
  292.2 2.2 convert_element_type.60
  294.4 299.6 %reduce-scatter.5.cloned.1.call-done = f32[256,2,1,128]{3,0,2,1:T(8,128)} async-done(((f32[8192,2,1,128]{3,0,2,1:T(8,128)}), f32[256,2,1,128]{3,0,2,1:T(8,128)}) %reduce-scatter.5.cloned.1.call-update) | async-done | bytes 262160 | tf_op jit(solution)/shard_map/reduce_scatter | solution.py:174
  594.1 1.0 convert.4
  595.1 0.7 slice_bitcast_fusion
  (25 shorter events, 0.9 us)
Async XLA Ops:
  7.2 38.2 %all-gather.8.cloned.1.call-start = ((), (), s32[]{:S(2)}) async-start(), calls=%async_computation.5 | async-start | bytes 3276800 | tf_op jit(solution)/shard_map/all_gather | solution.py:142
  7.9 112.5 %all-gather.6.cloned.1.call-start = ((), (), s32[]{:S(2)}) async-start(), calls=%async_computation.3 | async-start | bytes 2162688 | tf_op jit(solution)/shard_map/all_gather | solution.py:120
  8.6 182.5 %all-gather.4.cloned.1.call-start = ((), (), s32[]{:S(2)}) async-start(), calls=%async_computation.2 | async-start | bytes 2162688 | tf_op jit(solution)/shard_map/all_gather | solution.py:121
  9.4 282.8 %reduce-scatter.3.cloned.1.call-start = ((), (), s32[]{:S(2)}) async-start(), calls=%async_computation.4 | async-start | bytes 6553600 | tf_op jit(solution)/shard_map/reduce_scatter | solution.py:135
  202.8 391.3 %reduce-scatter.5.cloned.1.call-start = ((), (), s32[]{:S(2)}) async-start(), calls=%async_computation.6 | async-start | bytes 8650752 | tf_op jit(solution)/shard_map/reduce_scatter | solution.py:174
Sparse Core Ops, SparseCore 0:
  9.7 35.6 all-gather.7
  48.3 72.0 all-gather.5
  123.4 67.6 all-gather.3
  202.9 89.2 reduce-scatter.2
  294.5 299.5 reduce-scatter.4
where the time goes:
time: 605 us; the launch traced here: 602 us
  waiting for transfers between devices  543 us (90%)
  matrix products  27.7 us (5%)
  between operations  16.5 us (3%)
  local copies, waits for them, and re-layouts  7.38 us (1%)
  other arithmetic  7.19 us (1%)
    reduce_scatter x1, waiting for transfers between devices, local(): key_own = lax.psum_scatter(key_sum, 'ctx', scatter_dimension=0, tiled=True)  300 us
    reduce_scatter x1, waiting for transfers between devices, local(): lax.psum_scatter(jnp.dot(attn_flat, out_weight, preferred_element_type=jn...  75 us
    all_gather x1, waiting for transfers between devices, local(): lax.all_gather(value_matrix, 'ctx', axis=0, tiled=True)  68 us
    all_gather x1, waiting for transfers between devices, local(): lax.all_gather(key_rows, 'ctx', axis=0, tiled=True)  66.9 us
    all_gather x1, waiting for transfers between devices, local(): lax.all_gather(cotangent, 'head', axis=0, tiled=True)  31.6 us
  transfers between devices with their start and end apart: 5, of which 5 were waited for; matrix products, arithmetic and copies ran while one was open for 5% of the time, Pallas kernels for 0%

commit v1 on v0

v1 whole, which is shorter than its diff:
```python
import functools
import math

import jax
import jax.numpy as jnp
from jax import lax
from jax.experimental import pallas as pl
from jax.experimental.pallas import tpu as pltpu
from jax.sharding import PartitionSpec as P

BF = jnp.bfloat16
F32 = jnp.float32
MESH = pl.DeviceIdType.MESH
YS, ZS, XS = 2, 4, 4
NCTX = YS * ZS * XS
HEAD = 128
GROUP = 8
BLOCK = 256
UNIT = 256
UNIT_POS = UNIT // GROUP
OWN = BLOCK * GROUP // UNIT
GIVE = 4
WORK = (OWN + GIVE) * UNIT
LOW = -1e30
VMEM_LIMIT = 60 * 1024 * 1024

NT = (((1,), (1,)), ((), ()))
NN = (((1,), (0,)), ((), ()))
TN = (((0,), (0,)), ((), ()))


def dot(a, b, dims):
    return lax.dot_general(a, b, dims, preferred_element_type=F32)


def share():
    c = lax.axis_index("ctx")
    low = jnp.minimum(c, NCTX - 1 - c)
    given = jnp.where(
        low <= 2, 4, jnp.where(low <= 8, 3, jnp.where(low <= 11, 2, jnp.where(low <= 14, 1, 0)))
    )
    return c, c < NCTX // 2, given


def place():
    c = lax.axis_index("ctx")
    return c // (ZS * XS), (c // XS) % ZS, c % XS


def ctx_of(y, z, x):
    return (y * ZS + z) * XS + x


def neighbours():
    y, z, x = place()
    xs = [ctx_of(y, z, (x + d) % XS) for d in (1, XS - 1)]
    zs = [ctx_of(y, (z + d) % ZS, x) for d in (1, ZS - 1)]
    return ctx_of(1 - y, z, x), xs, zs


def greet(ctx_list, head_list):
    barrier = pltpu.get_barrier_semaphore()
    for other in ctx_list:
        pl.semaphore_signal(barrier, inc=1, device_id={"ctx": other}, device_id_type=MESH)
    for other in head_list:
        pl.semaphore_signal(barrier, inc=1, device_id={"head": other}, device_id_type=MESH)
    pl.semaphore_wait(barrier, len(ctx_list) + len(head_list))


class Courier:
    def __init__(self, send, recv):
        self.send, self.recv, self.made = send, recv, {}

    def plan(self, name, axis, other, src, dst):
        n = len(self.made)
        self.made[name] = lambda: pltpu.make_async_remote_copy(
            src_ref=src,
            dst_ref=dst,
            send_sem=self.send.at[n],
            recv_sem=self.recv.at[n],
            device_id={axis: other},
            device_id_type=MESH,
        )

    def go(self, *names):
        for name in names:
            self.made[name]().start()

    def got(self, *names):
        for name in names:
            self.made[name]().wait_recv()

    def finish(self):
        for copy in self.made.values():
            copy().wait_send()


class Handover:
    def __init__(self, send, recv, src, src_unit, dst, dst_unit, from_low):
        c, is_low, given = share()
        self.given = given
        self.sends = is_low if from_low else jnp.logical_not(is_low)
        self.takes = jnp.logical_not(self.sends)

        def copy(i):
            return pltpu.make_async_remote_copy(
                src_ref=src.at[pl.ds((src_unit + i) * UNIT, UNIT)],
                dst_ref=dst.at[pl.ds((dst_unit + i) * UNIT, UNIT)],
                send_sem=send.at[i],
                recv_sem=recv.at[i],
                device_id={"ctx": NCTX - 1 - c},
                device_id_type=MESH,
            )

        self.copy = copy

    def each(self, who, act):
        for i in range(GIVE):

            @pl.when(jnp.logical_and(who, i < self.given))
            def _():
                act(i)

    def start(self):
        self.each(self.sends, lambda i: self.copy(i).start())

    def wait_recv(self):
        self.each(self.takes, lambda i: self.copy(i).wait_recv())

    def wait_send(self):
        self.each(self.sends, lambda i: self.copy(i).wait_send())


def tail_of(x):
    one = x.astype(BF).astype(F32)
    rest = x - one
    two = rest.astype(BF).astype(F32)
    three = rest - two
    lane = lax.broadcasted_iota(jnp.int32, x.shape, 1)
    return jnp.where(
        lane == 0, -one, jnp.where(lane == 1, -two, jnp.where(lane == 2, -three, 0.0))
    ).astype(BF)


def layer_kernel(
    unit, scale,
    k_ref, v_ref, cot_ref, q_ref, w_hbm,
    dq_ref, gk_ref, gv_ref, o_ref,
    w_ref, wsem, kv_ref, ca_ref, qw_ref, ga_ref, attn_ref, m_row, l_row, acc_ref,
    attn_far, dq_par, dq_far, af_ref, flat_ref, opart, ocore, osum, orow,
    qx_ref, gx_ref, kx_ref, vx_ref, dqs_ref, dk_ref, dv_ref,
    p_ref, t_ref, r_ref, m_ref, t2_ref, r2_ref, s_ref, y_ref,
    send, recv, hsend, hrecv,
):
    y, z, x = place()
    c, is_low, given = share()
    h = lax.axis_index("head")
    core, row = h ^ 1, h ^ 2
    mine, up = h % 2, h // 2
    partner, xs, zs = neighbours()
    w_copy = pltpu.make_async_copy(w_hbm, w_ref, wsem)
    w_copy.start()
    greet([partner] + xs + zs + [NCTX - 1 - c], [core, row])
    mail = Courier(send, recv)

    def hand(i, *what):
        return Handover(hsend.at[i], hrecv.at[i], *what)

    kv_ref[c, 0] = k_ref[...]
    kv_ref[c, 1] = v_ref[...]
    mail.plan("pair", "ctx", partner, kv_ref.at[c], kv_ref.at[c])
    mail.go("pair")
    qs = hand(0, q_ref, 0, qw_ref, OWN, False)
    gs = hand(1, ga_ref, 0, ga_ref, OWN, False)
    attn_home = hand(2, attn_ref, OWN, attn_far, 0, True)
    dq_home = hand(3, dq_par, 0, dq_far, 0, True)
    qs.start()
    ca_ref[h] = cot_ref[...]
    for name, o, i in (("cot row", row, h), ("cot core", core, h), ("cot relay", core, row)):
        mail.plan(name, "head", o, ca_ref.at[i], ca_ref.at[i])
    mail.go("cot row", "cot core")

    routes = ((z, x, zs, xs), (x, z, xs, zs))
    for n, (a, b, an, bn) in enumerate(routes):

        def slot(i, j, n=n):
            return kv_ref.at[jnp.where(n == 0, 16 + i * 4 + j, j * 4 + i)]

        for d in range(2):
            mail.plan((n, "beside", d), "ctx", an[d], slot(a, b), slot(a, b))
            part = slot((a + (3, 1)[d]) % 4, b).at[d]
            mail.plan((n, "on", d), "ctx", an[d], part, part)
            for s, off in enumerate((0, 3, 1, 2)):
                i = (a + off) % 4
                mail.plan((n, "third", s, d), "ctx", bn[d], slot(i, b), slot(i, b))
                part = slot(i, (b + (3, 1)[d]) % 4).at[d]
                mail.plan((n, "last", s, d), "ctx", bn[d], part, part)

    def pass_on(n, s):
        for d in range(2):
            mail.got((n, "third", s, d))
            mail.go((n, "last", s, d))

    for n, (a, an, b, bn) in enumerate(((x, xs, z, zs), (z, zs, x, xs))):
        steps = (
            (1, p_ref.at[n], a, an, t_ref.at[n], r_ref.at[n]),
            (2, m_ref.at[n], b, bn, t2_ref.at[n], r2_ref.at[n]),
        )
        for stage, piece, at, to, t, r in steps:
            for d in range(2):
                nxt = (at + (1, 3)[d]) % 4
                mail.plan((n, stage, "far", d), "ctx", to[d], piece.at[(at + 2) % 4, d], t.at[d])
                mail.plan(
                    (n, stage, "near", d), "ctx", to[d], piece.at[nxt, 1 - d], r.at[d, 1 - d]
                )
                mail.plan((n, stage, "sum", d), "ctx", to[d], t.at[d], r.at[d, d])
    mail.plan("y", "ctx", partner, s_ref.at[y], y_ref)
    for i in range(2):
        mail.plan(("core", i), "head", core, opart.at[2 * i + 1 - mine], ocore.at[i])
    mail.plan("row", "head", row, osum.at[1 - up], orow)

    def far(n, stage):
        mail.go((n, stage, "far", 0), (n, stage, "far", 1))

    def near(n, stage, d):
        mail.go((n, stage, "near", d))

    def relay(n, stage):
        piece, at, t = (
            (p_ref.at[n], (x, z)[n], t_ref.at[n])
            if stage == 1
            else (m_ref.at[n], (z, x)[n], t2_ref.at[n])
        )
        for d in range(2):
            nxt = (at + (1, 3)[d]) % 4
            mail.got((n, stage, "far", d))
            t[d] = (piece[nxt, d].astype(F32) + t[d].astype(F32)).astype(BF)
            mail.go((n, stage, "sum", d))

    def arrived(n, stage):
        for d in range(2):
            mail.got((n, stage, "near", d), (n, stage, "sum", d))

    def total_first(n):
        arrived(n, 1)
        at = (x, z)[n]
        for kv in range(2):
            for j in range(4):
                m_ref[n, j, kv] = (
                    p_ref[n, at, kv, j].astype(F32)
                    + r_ref[n, 0, kv, j].astype(F32)
                    + r_ref[n, 1, kv, j].astype(F32)
                ).astype(BF)
        far(n, 2)
        near(n, 2, 0)
        near(n, 2, 1)

    def total_second(n):
        arrived(n, 2)
        at = (z, x)[n]
        s_ref[n] = (
            m_ref[n, at].astype(F32) + r2_ref[n, 0].astype(F32) + r2_ref[n, 1].astype(F32)
        ).astype(BF)

    def output_projection():
        attn_home.wait_recv()
        own = OWN * UNIT
        af_ref[...] = attn_ref[pl.ds(0, own), :].astype(F32)

        def place_far(i):
            rows = pl.ds(i * UNIT, UNIT)
            af_ref[rows, :] = attn_far[rows, :].astype(F32)

        attn_home.each(attn_home.takes, place_far)
        for i in range(GROUP):
            flat_ref[:, i * HEAD : (i + 1) * HEAD] = af_ref[
                pl.ds(i, BLOCK, stride=GROUP), :
            ].astype(BF)
        wide = 512

        def chunk(n, carry):
            cols = pl.ds(pl.multiple_of(n * wide, wide), wide)
            part = dot(flat_ref[...], w_ref[:, cols], NN).astype(BF)
            opart[:, :, cols] = part.reshape(4, BLOCK // 4, wide)
            return carry

        lax.fori_loop(0, w_ref.shape[1] // wide, chunk, 0)
        mail.go(("core", 0), ("core", 1))

    def output_core():
        for i in range(2):
            mail.got(("core", i))
            osum[i] = (opart[2 * i + mine].astype(F32) + ocore[i].astype(F32)).astype(BF)
        mail.go("row")

    begin = jnp.where(is_low, 0, given)
    taken = OWN + jnp.where(is_low, given, 0)

    def block_of(n, at, j):
        return jnp.where(n == 0, 16 + 4 * j + at, 4 * at + j)

    def over_group(n, at, tile, between=None):
        def row_set(own, carry):
            mine_now = own == 1
            u0 = jnp.where(mine_now, begin, OWN)
            u1 = jnp.where(mine_now, OWN, taken)
            qb = jnp.where(mine_now, c, NCTX - 1 - c)
            pos0 = jnp.where(mine_now, 0, OWN)
            twos = (u1 - u0) // 2
            odd = (u1 - u0) % 2

            def key_pair(jp, carry):
                whole = qb > block_of(n, at, 2 * jp + 1)

                def full(i, carry):
                    tile(u0 + 2 * i, 2, 2 * jp, 2, None)
                    return carry

                lax.fori_loop(0, jnp.where(whole, twos, 0), full, 0)

                @pl.when(jnp.logical_and(whole, odd == 1))
                def _():
                    tile(u1 - 1, 1, 2 * jp, 2, None)

                def single_block(j, carry):
                    ahead = (qb - block_of(n, at, j)) * BLOCK
                    some = jnp.logical_and(jnp.logical_not(whole), ahead >= 0)

                    def part(i, carry):
                        u = u0 + 2 * i
                        tile(u, 2, j, 1, ahead + (u - pos0) * UNIT_POS)
                        return carry

                    lax.fori_loop(0, jnp.where(some, twos, 0), part, 0)

                    @pl.when(jnp.logical_and(some, odd == 1))
                    def _():
                        u = u1 - 1
                        tile(u, 1, j, 1, ahead + (u - pos0) * UNIT_POS)

                    return carry

                lax.fori_loop(2 * jp, 2 * jp + 2, single_block, 0)
                return carry

            lax.fori_loop(0, 2, key_pair, 0)
            if between is not None:
                between(own)
            return carry

        lax.fori_loop(0, 2, row_set, 0)

    def rows_of(first, units):
        return pl.ds(pl.multiple_of(first * UNIT, UNIT), units * UNIT)

    def mask(keys, n, ahead):
        qpos = ahead + lax.broadcasted_iota(jnp.int32, (keys, n), 1) // GROUP
        return lax.broadcasted_iota(jnp.int32, (keys, n), 0) <= qpos

    def forward_group(s, carry):
        n = 1 - s % 2
        i = s // 2
        off = jnp.where(i == 0, 0, jnp.where(i == 1, 3, jnp.where(i == 2, 1, 2)))
        at = (jnp.where(n == 0, x, z) + off) % 4

        @pl.when(s == 1)
        def _():
            for step in range(2):
                pass_on(1, step)
                pass_on(0, step)

        @pl.when(s == 2)
        def _():
            pass_on(1, 2)
            pass_on(1, 3)
            mail.got("cot row")
            mail.go("cot relay")

        @pl.when(s == 3)
        def _():
            pass_on(0, 2)
            pass_on(0, 3)

        @pl.when(s == 5)
        def _():
            project_cotangent()

        for n_now in range(2):

            @pl.when(s == 7 - n_now)
            def _():
                for step in range(4):
                    mail.got((n_now, "last", step, 0), (n_now, "last", step, 1))

        def tile(first, units, j, blocks, ahead):
            rows = rows_of(first, units)
            held = [block_of(n, at, j + i) for i in range(blocks)]
            keys = jnp.concatenate([kv_ref[b, 0] for b in held], axis=0)
            values = jnp.concatenate([kv_ref[b, 1] for b in held], axis=0)
            sc = dot(keys, qw_ref[rows, :], NT)
            if ahead is not None:
                sc = jnp.where(mask(sc.shape[0], sc.shape[1], ahead), sc, LOW)
            top = m_row[:, rows]
            new = jnp.maximum(top, jnp.max(sc, axis=0, keepdims=True))
            alpha = jnp.exp2((top - new) * unit)
            p = jnp.exp2((sc - new) * unit)
            m_row[:, rows] = new
            l_row[:, rows] = l_row[:, rows] * alpha + jnp.sum(p, axis=0, keepdims=True)
            acc_ref[:, rows] = acc_ref[:, rows] * alpha + dot(values, p.astype(BF), TN)

        over_group(n, at, tile)
        return carry

    def project_cotangent():
        mail.got("cot core", "cot relay")
        w_copy.wait()

        def project(n, carry):
            wide = 1024
            total = jnp.zeros((BLOCK, 2 * HEAD), F32)
            for i in range(cot_ref.shape[1] // wide):
                cols = pl.ds(i * wide, wide)
                total += dot(
                    ca_ref[:, :, cols].reshape(BLOCK, wide),
                    w_ref[pl.ds(pl.multiple_of(n * 2 * HEAD, 2 * HEAD), 2 * HEAD), cols],
                    NT,
                )
            for i in range(2):
                af_ref[pl.ds(2 * n + i, BLOCK, stride=GROUP), :] = total[
                    :, i * HEAD : (i + 1) * HEAD
                ]
            return carry

        lax.fori_loop(0, GROUP // 2, project, 0)
        ga_ref[pl.ds(0, OWN * UNIT), :] = af_ref[...].astype(BF)
        gs.start()

    qw_ref[pl.ds(0, OWN * UNIT), :] = q_ref[...]
    m_row[...] = jnp.full_like(m_row, LOW)
    l_row[...] = jnp.zeros_like(l_row)
    acc_ref[...] = jnp.zeros_like(acc_ref)
    mail.got("pair")
    for n in range(2):
        mail.go((n, "beside", 0), (n, "beside", 1), (n, "third", 0, 0), (n, "third", 0, 1))
    for n in range(2):
        for d in range(2):
            mail.got((n, "beside", d))
            mail.go((n, "on", d), (n, "third", 1 + d, 0), (n, "third", 1 + d, 1))
    for n in range(2):
        mail.got((n, "on", 0), (n, "on", 1))
        mail.go((n, "third", 3, 0), (n, "third", 3, 1))
    qs.wait_recv()
    lax.fori_loop(0, 8, forward_group, 0)

    def finish_forward(i, carry):
        rows = pl.ds(pl.multiple_of(i * 512, 512), 512)
        l = l_row[:, rows]
        attn_ref[rows, :] = jnp.transpose(acc_ref[:, rows] / l).astype(BF)
        lse = m_row[:, rows] + jnp.log2(l) / unit
        one = lse.astype(BF).astype(F32)
        rest = lse - one
        two = rest.astype(BF).astype(F32)
        three = rest - two
        which = lax.broadcasted_iota(jnp.int32, (HEAD, 512), 0)
        pieces = jnp.where(
            which == 0, -one, jnp.where(which == 1, -two, jnp.where(which == 2, -three, 0.0))
        )
        qx_ref[rows, :HEAD] = qw_ref[rows, :]
        qx_ref[rows, HEAD:] = jnp.transpose(pieces).astype(BF)
        return carry

    lax.fori_loop(0, WORK // 512, finish_forward, 0)
    attn_home.start()
    gs.wait_recv()

    def prepare(i, carry):
        rows = pl.ds(pl.multiple_of(i * 512, 512), 512)
        ga = ga_ref[rows, :]
        delta = jnp.sum(ga.astype(F32) * attn_ref[rows, :].astype(F32), axis=1, keepdims=True)
        gx_ref[rows, :HEAD] = ga
        gx_ref[rows, HEAD:] = tail_of(jnp.broadcast_to(delta, (512, HEAD)))
        dqs_ref[rows, :] = jnp.zeros((512, HEAD), F32)
        return carry

    lax.fori_loop(0, WORK // 512, prepare, 0)
    lane = lax.broadcasted_iota(jnp.int32, (4 * BLOCK, HEAD), 1)
    ones = jnp.where(lane < 3, 1.0, 0.0).astype(BF)
    kx_ref[:, HEAD:] = ones
    vx_ref[:, HEAD:] = ones

    def backward_group(s, carry):
        n = s % 2
        i = s // 2
        off = jnp.where(i == 0, 2, jnp.where(i == 1, 1, jnp.where(i == 2, 3, 0)))
        at = (jnp.where(n == 0, x, z) + off) % 4

        for j in range(4):
            ks = pl.ds(j * BLOCK, BLOCK)
            kx_ref[ks, :HEAD] = kv_ref[block_of(n, at, j), 0]
            vx_ref[ks, :HEAD] = kv_ref[block_of(n, at, j), 1]
        dk_ref[...] = jnp.zeros_like(dk_ref)
        dv_ref[...] = jnp.zeros_like(dv_ref)

        def tile(first, units, j, blocks, ahead):
            rows = rows_of(first, units)
            ks = pl.ds(pl.multiple_of(j * BLOCK, BLOCK), blocks * BLOCK)
            p = jnp.exp2(dot(kx_ref[ks, :], qx_ref[rows, :], NT) * unit)
            if ahead is not None:
                p = jnp.where(mask(p.shape[0], p.shape[1], ahead), p, 0.0)
            g = dot(vx_ref[ks, :], gx_ref[rows, :], NT)
            ds = (p * g).astype(BF)
            dv_ref[ks, :] += dot(p.astype(BF), gx_ref[rows, :HEAD], NN)
            dk_ref[ks, :] += dot(ds, qx_ref[rows, :HEAD], NN)
            dqs_ref[rows, :] += dot(ds, kx_ref[ks, :HEAD], TN)

        def between(own):
            @pl.when(jnp.logical_and(s == 7, own == 0))
            def _():
                dq_par[...] = (dqs_ref[pl.ds(OWN * UNIT, GIVE * UNIT), :] * scale).astype(BF)
                dq_home.start()

        over_group(n, at, tile, between)
        for j in range(4):
            ks = pl.ds(j * BLOCK, BLOCK)
            p_ref[n, at, 0, j] = (dk_ref[ks, :] * scale).astype(BF)
            p_ref[n, at, 1, j] = dv_ref[ks, :].astype(BF)

        @pl.when(s == 0)
        def _():
            far(0, 1)

        @pl.when(s == 1)
        def _():
            far(1, 1)

        @pl.when(s == 2)
        def _():
            near(0, 1, 0)
            output_projection()

        @pl.when(s == 3)
        def _():
            near(1, 1, 0)

        @pl.when(s == 4)
        def _():
            near(0, 1, 1)
            relay(0, 1)
            output_core()

        @pl.when(s == 5)
        def _():
            near(1, 1, 1)
            relay(1, 1)

        @pl.when(s == 6)
        def _():
            total_first(0)

        return carry

    lax.fori_loop(0, 8, backward_group, 0)
    total_first(1)
    relay(0, 2)
    dq_ref[...] = (dqs_ref[pl.ds(0, OWN * UNIT), :] * scale).astype(BF)
    relay(1, 2)
    total_second(0)

    @pl.when(y == 0)
    def _():
        mail.go("y")

    total_second(1)

    @pl.when(y == 1)
    def _():
        mail.go("y")

    mail.got("row")
    o_ref[...] = (osum[up].astype(F32) + orow[...].astype(F32)).astype(BF)
    dq_home.wait_recv()

    def place_dq(i):
        rows = pl.ds(i * UNIT, UNIT)
        dq_ref[rows, :] = dq_far[rows, :]

    dq_home.each(dq_home.takes, place_dq)
    mail.got("y")
    gk_ref[...] = (s_ref[1 - y, 0].astype(F32) + y_ref[0].astype(F32)).astype(BF)
    gv_ref[...] = (s_ref[1 - y, 1].astype(F32) + y_ref[1].astype(F32)).astype(BF)
    mail.finish()
    for hand in (qs, gs, attn_home, dq_home):
        hand.wait_send()


COPIES = 1 + 3 + 2 * 20 + 2 * 2 * 6 + 1 + 3


def layer(unit, scale, k, v, cot, q, w):
    vm, dma = pltpu.VMEM, pltpu.SemaphoreType.DMA
    part = (BLOCK // 4, w.shape[1])
    return pl.pallas_call(
        functools.partial(layer_kernel, unit, scale),
        out_shape=(
            jax.ShapeDtypeStruct((OWN * UNIT, HEAD), BF),
            jax.ShapeDtypeStruct((BLOCK, HEAD), BF),
            jax.ShapeDtypeStruct((BLOCK, HEAD), BF),
            jax.ShapeDtypeStruct(part, BF),
        ),
        in_specs=vmem_specs(4) + [pl.BlockSpec(memory_space=pl.ANY)],
        out_specs=tuple(vmem_specs(4)),
        scratch_shapes=[
            vm(w.shape, BF),
            dma,
            vm((NCTX, 2, BLOCK, HEAD), BF),
            vm((4,) + cot.shape, BF),
            vm((WORK, HEAD), BF),
            vm((WORK, HEAD), BF),
            vm((WORK, HEAD), BF),
            vm((1, WORK), F32),
            vm((1, WORK), F32),
            vm((HEAD, WORK), F32),
            vm((GIVE * UNIT, HEAD), BF),
            vm((GIVE * UNIT, HEAD), BF),
            vm((GIVE * UNIT, HEAD), BF),
            vm((OWN * UNIT, HEAD), F32),
            vm((BLOCK, GROUP * HEAD), BF),
            vm((4,) + part, BF),
            vm((2,) + part, BF),
            vm((2,) + part, BF),
            vm(part, BF),
            vm((WORK, 2 * HEAD), BF),
            vm((WORK, 2 * HEAD), BF),
            vm((4 * BLOCK, 2 * HEAD), BF),
            vm((4 * BLOCK, 2 * HEAD), BF),
            vm((WORK, HEAD), F32),
            vm((4 * BLOCK, HEAD), F32),
            vm((4 * BLOCK, HEAD), F32),
            vm((2, 4, 2, 4, BLOCK, HEAD), BF),
            vm((2, 2, 4, BLOCK, HEAD), BF),
            vm((2, 2, 2, 4, BLOCK, HEAD), BF),
            vm((2, 4, 2, BLOCK, HEAD), BF),
            vm((2, 2, BLOCK, HEAD), BF),
            vm((2, 2, 2, BLOCK, HEAD), BF),
            vm((2, 2, BLOCK, HEAD), BF),
            vm((2, BLOCK, HEAD), BF),
            dma((COPIES,)),
            dma((COPIES,)),
            dma((4, GIVE)),
            dma((4, GIVE)),
        ],
        compiler_params=pltpu.CompilerParams(
            collective_id=0, has_side_effects=True, vmem_limit_bytes=VMEM_LIMIT
        ),
        name="layer",
    )(k, v, cot, q, w)


def vmem_specs(n):
    return [pl.BlockSpec(memory_space=pltpu.VMEM)] * n


def local(queries, key_rows, value_matrix, out_weight, cotangent):
    rows, heads, head = queries.shape
    scale = 1.0 / math.sqrt(head)
    unit = scale * math.log2(math.e)
    grad_queries, grad_keys, grad_values, output = layer(
        unit,
        scale,
        key_rows.reshape(rows, head),
        value_matrix.reshape(rows, head),
        cotangent,
        queries.reshape(rows * heads, head),
        out_weight,
    )
    return (
        output,
        grad_queries.reshape(rows, heads, head),
        grad_keys.reshape(rows, 1, head),
        grad_values.reshape(rows, 1, head),
    )


def solution(mesh):
    return jax.shard_map(
        local,
        mesh=mesh,
        in_specs=(
            P("ctx", "head", None),
            P("ctx", "head", None),
            P("ctx", "head", None),
            P("head", None),
            P(("ctx", "head"), None),
        ),
        out_specs=(
            P(("ctx", "head"), None),
            P("ctx", "head", None),
            P("ctx", "head", None),
            P("ctx", "head", None),
        ),
        check_vma=False,
    )
```

time: 605 us -> 140 us (0.23)
  the two profiles are of different devices: /device:TPU:0 before, /device:TPU:98 now
where the time goes in v1:
time: 140 us; the launch traced here: 139 us
  Pallas kernels  132 us (94%)
  local copies, waits for them, and re-layouts  6.78 us (5%)
    pallas_call x1, Pallas kernels, layer(): pl.pallas_call(functools.partial(layer_kernel, unit, scale), out_shape=(j...  132 us
    unnamed x4, local copies, waits for them, and re-layouts  6.78 us

profile of v1, /device:TPU:98, one launch (start us, length us, event | category | flops | bytes accessed | tf_op | source)
XLA Modules:
  0.0 139.3 jit_solution(14578340416727331764)
XLA Ops:
  0.6 131.9 %layer.1 = (bf16[2048,128]{1,0:T(8,128)(2,1)}, bf16[256,128]{1,0:T(8,128)(2,1)}, bf16[256,128]{1,0:T(8,128)(2,1)}, bf16[64,5120]{1,0:T(8,128)(2,1)}) custom-call(bf16[256,128]{1,0:T(8,128)(2,1)} %bitcast.8, bf16[256,128]{1,0:T(8,128)(2,1)} %bitcast.9, bf16[64,5120]{1,0:T(8,128)(2,1)} %cot_ref.1, bf16[2048,128]{1,0:T(8,128)(2,1)} %bitcast.6, ...), custom_call_target="tpu_custom_call" | custom-call | tf_op jit(solution)/shard_map/layer/pallas_call | solution.py:602
  132.6 2.0 %copy.13 = bf16[64,5120]{1,0:T(8,128)(2,1)} copy(bf16[64,5120]{1,0:T(8,128)(2,1)} %get-tuple-element.16) | data formatting | bytes 1310720
  134.5 1.9 %copy.14 = bf16[256,8,128]{2,1,0:T(8,128)(2,1)} copy(bf16[256,8,128]{2,1,0:T(8,128)(2,1)} %bitcast.7) | data formatting | bytes 1048576
  136.4 1.5 %copy.15 = bf16[256,1,128]{2,0,1:T(8,128)(2,1)} copy(bf16[256,1,128]{2,0,1:T(8,128)(2,1)} %bitcast.11) | data formatting | bytes 131072
  137.9 1.5 %copy.16 = bf16[256,1,128]{2,0,1:T(8,128)(2,1)} copy(bf16[256,1,128]{2,0,1:T(8,128)(2,1)} %bitcast.10) | data formatting | bytes 131072

commit v2 on v1

--- a/solution.py
+++ b/solution.py
@@ -146,7 +146,7 @@
     unit, scale,
     k_ref, v_ref, cot_ref, q_ref, w_hbm,
     dq_ref, gk_ref, gv_ref, o_ref,
-    w_ref, wsem, kv_ref, ca_ref, qw_ref, ga_ref, attn_ref, m_row, l_row, acc_ref,
+    w_ref, wsem, kv_ref, ca_ref, gt_ref, qw_ref, ga_ref, attn_ref, m_row, l_row, acc_ref,
     attn_far, dq_par, dq_far, af_ref, flat_ref, opart, ocore, osum, orow,
     qx_ref, gx_ref, kx_ref, vx_ref, dqs_ref, dk_ref, dv_ref,
     p_ref, t_ref, r_ref, m_ref, t2_ref, r2_ref, s_ref, y_ref,
@@ -178,7 +178,6 @@
     ca_ref[h] = cot_ref[...]
     for name, o, i in (("cot row", row, h), ("cot core", core, h), ("cot relay", core, row)):
         mail.plan(name, "head", o, ca_ref.at[i], ca_ref.at[i])
-    mail.go("cot row", "cot core")
 
     routes = ((z, x, zs, xs), (x, z, xs, zs))
     for n, (a, b, an, bn) in enumerate(routes):
@@ -299,53 +298,48 @@
     def block_of(n, at, j):
         return jnp.where(n == 0, 16 + 4 * j + at, 4 * at + j)
 
-    def over_group(n, at, tile, between=None):
-        def row_set(own, carry):
-            mine_now = own == 1
+    def over_group(n, at, tile, own_first, between):
+        def row_set(turn, carry):
+            mine_now = turn == (0 if own_first else 1)
             u0 = jnp.where(mine_now, begin, OWN)
             u1 = jnp.where(mine_now, OWN, taken)
             qb = jnp.where(mine_now, c, NCTX - 1 - c)
             pos0 = jnp.where(mine_now, 0, OWN)
-            twos = (u1 - u0) // 2
-            odd = (u1 - u0) % 2
+            count = u1 - u0
 
             def key_pair(jp, carry):
                 whole = qb > block_of(n, at, 2 * jp + 1)
 
-                def full(i, carry):
-                    tile(u0 + 2 * i, 2, 2 * jp, 2, None)
-                    return carry
-
-                lax.fori_loop(0, jnp.where(whole, twos, 0), full, 0)
-
-                @pl.when(jnp.logical_and(whole, odd == 1))
-                def _():
-                    tile(u1 - 1, 1, 2 * jp, 2, None)
+                def rows(on, j, blocks, ahead):
+                    def many(i, carry):
+                        tile(u0 + 4 * i, (2, 2), j, blocks, ahead, u0 + 4 * i - pos0)
+                        return carry
+
+                    lax.fori_loop(0, jnp.where(on, count // 4, 0), many, 0)
+                    rest = jnp.where(on, count % 4, 0)
+                    for k, chains in ((3, (2, 1)), (2, (1, 1)), (1, (1,))):
+
+                        @pl.when(rest == k)
+                        def _():
+                            tile(u1 - k, chains, j, blocks, ahead, u1 - k - pos0)
+
+                rows(whole, 2 * jp, 2, None)
 
                 def single_block(j, carry):
                     ahead = (qb - block_of(n, at, j)) * BLOCK
                     some = jnp.logical_and(jnp.logical_not(whole), ahead >= 0)
-
-                    def part(i, carry):
-                        u = u0 + 2 * i
-                        tile(u, 2, j, 1, ahead + (u - pos0) * UNIT_POS)
-                        return carry
-
-                    lax.fori_loop(0, jnp.where(some, twos, 0), part, 0)
-
-                    @pl.when(jnp.logical_and(some, odd == 1))
-                    def _():
-                        u = u1 - 1
-                        tile(u, 1, j, 1, ahead + (u - pos0) * UNIT_POS)
-
+                    rows(some, j, 1, ahead)
                     return carry
 
                 lax.fori_loop(2 * jp, 2 * jp + 2, single_block, 0)
                 return carry
 
             lax.fori_loop(0, 2, key_pair, 0)
-            if between is not None:
-                between(own)
+
+            @pl.when(turn == 0)
+            def _():
+                between()
+
             return carry
 
         lax.fori_loop(0, 2, row_set, 0)
@@ -358,98 +352,116 @@
         return lax.broadcasted_iota(jnp.int32, (keys, n), 0) <= qpos
 
     def forward_group(s, carry):
-        n = 1 - s % 2
+        n = (1 - y + s) % 2
         i = s // 2
         off = jnp.where(i == 0, 0, jnp.where(i == 1, 3, jnp.where(i == 2, 1, 2)))
         at = (jnp.where(n == 0, x, z) + off) % 4
 
         @pl.when(s == 1)
         def _():
-            for step in range(2):
-                pass_on(1, step)
-                pass_on(0, step)
+            each_pass(True, lambda n: (pass_on(n, 0), pass_on(n, 1)))
 
         @pl.when(s == 2)
         def _():
-            pass_on(1, 2)
-            pass_on(1, 3)
+            each_pass(True, lambda n: (pass_on(n, 2), pass_on(n, 3)))
+            each_pass(False, lambda n: (pass_on(n, 0), pass_on(n, 1)))
             mail.got("cot row")
             mail.go("cot relay")
 
         @pl.when(s == 3)
         def _():
-            pass_on(0, 2)
-            pass_on(0, 3)
+            each_pass(False, lambda n: (pass_on(n, 2), pass_on(n, 3)))
 
         @pl.when(s == 5)
         def _():
             project_cotangent()
 
-        for n_now in range(2):
-
-            @pl.when(s == 7 - n_now)
-            def _():
-                for step in range(4):
-                    mail.got((n_now, "last", step, 0), (n_now, "last", step, 1))
-
-        def tile(first, units, j, blocks, ahead):
-            rows = rows_of(first, units)
+        def arrived_last(n):
+            for step in range(4):
+                mail.got((n, "last", step, 0), (n, "last", step, 1))
+
+        @pl.when(s == 6)
+        def _():
+            each_pass(True, arrived_last)
+
+        @pl.when(s == 7)
+        def _():
+            each_pass(False, arrived_last)
+
+        def tile(first, chains, j, blocks, ahead, unit_at):
             held = [block_of(n, at, j + i) for i in range(blocks)]
             keys = jnp.concatenate([kv_ref[b, 0] for b in held], axis=0)
             values = jnp.concatenate([kv_ref[b, 1] for b in held], axis=0)
-            sc = dot(keys, qw_ref[rows, :], NT)
-            if ahead is not None:
-                sc = jnp.where(mask(sc.shape[0], sc.shape[1], ahead), sc, LOW)
-            top = m_row[:, rows]
-            new = jnp.maximum(top, jnp.max(sc, axis=0, keepdims=True))
-            alpha = jnp.exp2((top - new) * unit)
-            p = jnp.exp2((sc - new) * unit)
-            m_row[:, rows] = new
-            l_row[:, rows] = l_row[:, rows] * alpha + jnp.sum(p, axis=0, keepdims=True)
-            acc_ref[:, rows] = acc_ref[:, rows] * alpha + dot(values, p.astype(BF), TN)
-
-        over_group(n, at, tile)
+            offsets = [sum(chains[:i]) for i in range(len(chains))]
+            sets = [rows_of(first + o, units) for o, units in zip(offsets, chains)]
+            scores = [dot(keys, qw_ref[rows, :], NT) for rows in sets]
+            for rows, o, sc in zip(sets, offsets, scores):
+                if ahead is not None:
+                    past = ahead + (unit_at + o) * UNIT_POS
+                    sc = jnp.where(mask(sc.shape[0], sc.shape[1], past), sc, LOW)
+                top = m_row[:, rows]
+                new = jnp.maximum(top, jnp.max(sc, axis=0, keepdims=True))
+                alpha = jnp.exp2((top - new) * unit)
+                p = jnp.exp2((sc - new) * unit)
+                m_row[:, rows] = new
+                l_row[:, rows] = l_row[:, rows] * alpha + jnp.sum(p, axis=0, keepdims=True)
+                acc_ref[:, rows] = acc_ref[:, rows] * alpha + dot(values, p.astype(BF), TN)
+
+        def between():
+            @pl.when(s == 0)
+            def _():
+                qs.wait_recv()
+
+        over_group(n, at, tile, True, between)
         return carry
 
     def project_cotangent():
         mail.got("cot core", "cot relay")
         w_copy.wait()
 
+        wide = 1024
+        gt_ref[...] = jnp.zeros_like(gt_ref)
+
         def project(n, carry):
-            wide = 1024
-            total = jnp.zeros((BLOCK, 2 * HEAD), F32)
-            for i in range(cot_ref.shape[1] // wide):
-                cols = pl.ds(i * wide, wide)
-                total += dot(
-                    ca_ref[:, :, cols].reshape(BLOCK, wide),
-                    w_ref[pl.ds(pl.multiple_of(n * 2 * HEAD, 2 * HEAD), 2 * HEAD), cols],
-                    NT,
-                )
-            for i in range(2):
-                af_ref[pl.ds(2 * n + i, BLOCK, stride=GROUP), :] = total[
-                    :, i * HEAD : (i + 1) * HEAD
-                ]
+            cols = pl.ds(pl.multiple_of(n * wide, wide), wide)
+            gt_ref[...] += dot(w_ref[:, cols], ca_ref[:, :, cols].reshape(BLOCK, wide), NT)
             return carry
 
-        lax.fori_loop(0, GROUP // 2, project, 0)
+        lax.fori_loop(0, w_ref.shape[1] // wide, project, 0)
+        for i in range(GROUP):
+            af_ref[pl.ds(i, BLOCK, stride=GROUP), :] = jnp.transpose(
+                gt_ref[i * HEAD : (i + 1) * HEAD, :]
+            )
         ga_ref[pl.ds(0, OWN * UNIT), :] = af_ref[...].astype(BF)
         gs.start()
 
+    def each_pass(first, act):
+        for n in range(2):
+
+            @pl.when(y == (1 - n if first else n))
+            def _():
+                act(n)
+
+    def start(n):
+        mail.go((n, "beside", 0), (n, "beside", 1), (n, "third", 0, 0), (n, "third", 0, 1))
+
+    def front(n):
+        for d in range(2):
+            mail.got((n, "beside", d))
+            mail.go((n, "on", d), (n, "third", 1 + d, 0), (n, "third", 1 + d, 1))
+        mail.got((n, "on", 0), (n, "on", 1))
+        mail.go((n, "third", 3, 0), (n, "third", 3, 1))
+
+    each_pass(True, start)
     qw_ref[pl.ds(0, OWN * UNIT), :] = q_ref[...]
     m_row[...] = jnp.full_like(m_row, LOW)
     l_row[...] = jnp.zeros_like(l_row)
     acc_ref[...] = jnp.zeros_like(acc_ref)
     mail.got("pair")
-    for n in range(2):
-        mail.go((n, "beside", 0), (n, "beside", 1), (n, "third", 0, 0), (n, "third", 0, 1))
-    for n in range(2):
-        for d in range(2):
-            mail.got((n, "beside", d))
-            mail.go((n, "on", d), (n, "third", 1 + d, 0), (n, "third", 1 + d, 1))
-    for n in range(2):
-        mail.got((n, "on", 0), (n, "on", 1))
-        mail.go((n, "third", 3, 0), (n, "third", 3, 1))
-    qs.wait_recv()
+    each_pass(False, start)
+    mail.go("cot row", "cot core")
+    each_pass(True, front)
+    each_pass(False, front)
     lax.fori_loop(0, 8, forward_group, 0)
 
     def finish_forward(i, carry):
@@ -501,25 +513,33 @@
         dk_ref[...] = jnp.zeros_like(dk_ref)
         dv_ref[...] = jnp.zeros_like(dv_ref)
 
-        def tile(first, units, j, blocks, ahead):
-            rows = rows_of(first, units)
+        def tile(first, chains, j, blocks, ahead, unit_at):
             ks = pl.ds(pl.multiple_of(j * BLOCK, BLOCK), blocks * BLOCK)
-            p = jnp.exp2(dot(kx_ref[ks, :], qx_ref[rows, :], NT) * unit)
-            if ahead is not None:
-                p = jnp.where(mask(p.shape[0], p.shape[1], ahead), p, 0.0)
-            g = dot(vx_ref[ks, :], gx_ref[rows, :], NT)
-            ds = (p * g).astype(BF)
-            dv_ref[ks, :] += dot(p.astype(BF), gx_ref[rows, :HEAD], NN)
-            dk_ref[ks, :] += dot(ds, qx_ref[rows, :HEAD], NN)
-            dqs_ref[rows, :] += dot(ds, kx_ref[ks, :HEAD], TN)
-
-        def between(own):
-            @pl.when(jnp.logical_and(s == 7, own == 0))
+            offsets = [sum(chains[:i]) for i in range(len(chains))]
+            sets = [rows_of(first + o, units) for o, units in zip(offsets, chains)]
+            scores = [dot(kx_ref[ks, :], qx_ref[rows, :], NT) for rows in sets]
+            grads = [dot(vx_ref[ks, :], gx_ref[rows, :], NT) for rows in sets]
+            dv, dk = 0.0, 0.0
+            for rows, o, sc, g in zip(sets, offsets, scores, grads):
+                p = jnp.exp2(sc * unit)
+                if ahead is not None:
+                    past = ahead + (unit_at + o) * UNIT_POS
+                    p = jnp.where(mask(p.shape[0], p.shape[1], past), p, 0.0)
+                ds = (p * g).astype(BF)
+                dv += dot(p.astype(BF), gx_ref[rows, :HEAD], NN)
+                dk += dot(ds, qx_ref[rows, :HEAD], NN)
+                dqs_ref[rows, :] += dot(ds, kx_ref[ks, :HEAD], TN)
+            dv_ref[ks, :] += dv
+            dk_ref[ks, :] += dk
+
+        def between():
+            @pl.when(s == 7)
             def _():
                 dq_par[...] = (dqs_ref[pl.ds(OWN * UNIT, GIVE * UNIT), :] * scale).astype(BF)
                 dq_home.start()
-
-        over_group(n, at, tile, between)
+                relay(0, 2)
+
+        over_group(n, at, tile, False, between)
         for j in range(4):
             ks = pl.ds(j * BLOCK, BLOCK)
             p_ref[n, at, 0, j] = (dk_ref[ks, :] * scale).astype(BF)
@@ -561,7 +581,6 @@
 
     lax.fori_loop(0, 8, backward_group, 0)
     total_first(1)
-    relay(0, 2)
     dq_ref[...] = (dqs_ref[pl.ds(0, OWN * UNIT), :] * scale).astype(BF)
     relay(1, 2)
     total_second(0)
@@ -614,6 +633,7 @@
             dma,
             vm((NCTX, 2, BLOCK, HEAD), BF),
             vm((4,) + cot.shape, BF),
+            vm((GROUP * HEAD, BLOCK), F32),
             vm((WORK, HEAD), BF),
             vm((WORK, HEAD), BF),
             vm((WORK, HEAD), BF),
@@ -656,6 +676,24 @@
     )(k, v, cot, q, w)
 
 
+def results_kernel(*refs):
+    n = len(refs) // 2
+    for i in range(n):
+        refs[n + i][...] = refs[i][...]
+
+
+def results(*arrays):
+    n = len(arrays)
+    return pl.pallas_call(
+        results_kernel,
+        out_shape=tuple(jax.ShapeDtypeStruct(a.shape, a.dtype) for a in arrays),
+        in_specs=vmem_specs(n),
+        out_specs=tuple(vmem_specs(n)),
+        compiler_params=pltpu.CompilerParams(vmem_limit_bytes=VMEM_LIMIT),
+        name="results",
+    )(*arrays)
+
+
 def vmem_specs(n):
     return [pl.BlockSpec(memory_space=pltpu.VMEM)] * n
 
@@ -664,7 +702,7 @@
     rows, heads, head = queries.shape
     scale = 1.0 / math.sqrt(head)
     unit = scale * math.log2(math.e)
-    grad_queries, grad_keys, grad_values, output = layer(
+    made = layer(
         unit,
         scale,
         key_rows.reshape(rows, head),
@@ -673,6 +711,7 @@
         queries.reshape(rows * heads, head),
         out_weight,
     )
+    grad_queries, grad_keys, grad_values, output = results(*made)
     return (
         output,
         grad_queries.reshape(rows, heads, head),

time: 140 us -> 138 us (0.986)
  the two profiles are of different devices: /device:TPU:98 before, /device:TPU:0 now
where the time goes in v2:
time: 138 us; the launch traced here: 136 us
  Pallas kernels  135 us (98%)
    pallas_call x1, Pallas kernels, layer(): pl.pallas_call(functools.partial(layer_kernel, unit, scale), out_shape=(j...  133 us

profile of v2, /device:TPU:0, one launch (start us, length us, event | category | flops | bytes accessed | tf_op | source)
XLA Modules:
  0.0 135.9 jit_solution(12120280762306851828)
XLA Ops:
  0.6 132.9 %layer.1 = (bf16[2048,128]{1,0:T(8,128)(2,1)}, bf16[256,128]{1,0:T(8,128)(2,1)}, bf16[256,128]{1,0:T(8,128)(2,1)}, bf16[64,5120]{1,0:T(8,128)(2,1)}) custom-call(bf16[256,128]{1,0:T(8,128)(2,1)} %bitcast.7, bf16[256,128]{1,0:T(8,128)(2,1)} %bitcast.8, bf16[64,5120]{1,0:T(8,128)(2,1)} %cot_ref.1, bf16[2048,128]{1,0:T(8,128)(2,1)} %bitcast.6, ...), custom_call_target="tpu_custom_call" | custom-call | tf_op jit(solution)/shard_map/layer/pallas_call | solution.py:621
  133.5 2.4 %results.1 = (bf16[2048,128]{1,0:T(8,128)(2,1)}, bf16[256,128]{1,0:T(8,128)(2,1)}, bf16[256,128]{1,0:T(8,128)(2,1)}, bf16[64,5120]{1,0:T(8,128)(2,1)}) custom-call(bf16[2048,128]{1,0:T(8,128)(2,1)} %get-tuple-element.12.refs_0_, bf16[256,128]{1,0:T(8,128)(2,1)} %get-tuple-element.13.refs_1_, bf16[256,128]{1,0:T(8,128)(2,1)} %get-tuple-element.14.refs_2_, ...), custom_call_target="tpu_custom_call" | custom-call | tf_op jit(solution)/shard_map/results/pallas_call | solution.py:687

commit v3 on v2

--- a/solution.py
+++ b/solution.py
@@ -26,7 +26,6 @@
 
 NT = (((1,), (1,)), ((), ()))
 NN = (((1,), (0,)), ((), ()))
-TN = (((0,), (0,)), ((), ()))
 
 
 def dot(a, b, dims):
@@ -148,7 +147,7 @@
     dq_ref, gk_ref, gv_ref, o_ref,
     w_ref, wsem, kv_ref, ca_ref, gt_ref, qw_ref, ga_ref, attn_ref, m_row, l_row, acc_ref,
     attn_far, dq_par, dq_far, af_ref, flat_ref, opart, ocore, osum, orow,
-    qx_ref, gx_ref, kx_ref, vx_ref, dqs_ref, dk_ref, dv_ref,
+    qx_ref, gx_ref, kx_ref, vx_ref, xt_ref, dqs_ref, dk_ref, dv_ref,
     p_ref, t_ref, r_ref, m_ref, t2_ref, r2_ref, s_ref, y_ref,
     send, recv, hsend, hrecv,
 ):
@@ -275,7 +274,7 @@
             flat_ref[:, i * HEAD : (i + 1) * HEAD] = af_ref[
                 pl.ds(i, BLOCK, stride=GROUP), :
             ].astype(BF)
-        wide = 512
+        wide = 1024
 
         def chunk(n, carry):
             cols = pl.ds(pl.multiple_of(n * wide, wide), wide)
@@ -365,12 +364,15 @@
         def _():
             each_pass(True, lambda n: (pass_on(n, 2), pass_on(n, 3)))
             each_pass(False, lambda n: (pass_on(n, 0), pass_on(n, 1)))
+
+        @pl.when(s == 3)
+        def _():
+            each_pass(False, lambda n: (pass_on(n, 2), pass_on(n, 3)))
+
+        @pl.when(s == 4)
+        def _():
             mail.got("cot row")
             mail.go("cot relay")
-
-        @pl.when(s == 3)
-        def _():
-            each_pass(False, lambda n: (pass_on(n, 2), pass_on(n, 3)))
 
         @pl.when(s == 5)
         def _():
@@ -388,10 +390,13 @@
         def _():
             each_pass(False, arrived_last)
 
+        for j in range(4):
+            xt_ref[:, j * BLOCK : (j + 1) * BLOCK] = jnp.transpose(kv_ref[block_of(n, at, j), 1])
+
         def tile(first, chains, j, blocks, ahead, unit_at):
             held = [block_of(n, at, j + i) for i in range(blocks)]
             keys = jnp.concatenate([kv_ref[b, 0] for b in held], axis=0)
-            values = jnp.concatenate([kv_ref[b, 1] for b in held], axis=0)
+            values = xt_ref[:, pl.ds(pl.multiple_of(j * BLOCK, BLOCK), blocks * BLOCK)]
             offsets = [sum(chains[:i]) for i in range(len(chains))]
             sets = [rows_of(first + o, units) for o, units in zip(offsets, chains)]
             scores = [dot(keys, qw_ref[rows, :], NT) for rows in sets]
@@ -405,7 +410,7 @@
                 p = jnp.exp2((sc - new) * unit)
                 m_row[:, rows] = new
                 l_row[:, rows] = l_row[:, rows] * alpha + jnp.sum(p, axis=0, keepdims=True)
-                acc_ref[:, rows] = acc_ref[:, rows] * alpha + dot(values, p.astype(BF), TN)
+                acc_ref[:, rows] = acc_ref[:, rows] * alpha + dot(values, p.astype(BF), NN)
 
         def between():
             @pl.when(s == 0)
@@ -453,13 +458,13 @@
         mail.go((n, "third", 3, 0), (n, "third", 3, 1))
 
     each_pass(True, start)
+    mail.go("cot row", "cot core")
     qw_ref[pl.ds(0, OWN * UNIT), :] = q_ref[...]
     m_row[...] = jnp.full_like(m_row, LOW)
     l_row[...] = jnp.zeros_like(l_row)
     acc_ref[...] = jnp.zeros_like(acc_ref)
     mail.got("pair")
     each_pass(False, start)
-    mail.go("cot row", "cot core")
     each_pass(True, front)
     each_pass(False, front)
     lax.fori_loop(0, 8, forward_group, 0)
@@ -491,7 +496,7 @@
         delta = jnp.sum(ga.astype(F32) * attn_ref[rows, :].astype(F32), axis=1, keepdims=True)
         gx_ref[rows, :HEAD] = ga
         gx_ref[rows, HEAD:] = tail_of(jnp.broadcast_to(delta, (512, HEAD)))
-        dqs_ref[rows, :] = jnp.zeros((512, HEAD), F32)
+        dqs_ref[:, rows] = jnp.zeros((HEAD, 512), F32)
         return carry
 
     lax.fori_loop(0, WORK // 512, prepare, 0)
@@ -510,6 +515,7 @@
             ks = pl.ds(j * BLOCK, BLOCK)
             kx_ref[ks, :HEAD] = kv_ref[block_of(n, at, j), 0]
             vx_ref[ks, :HEAD] = kv_ref[block_of(n, at, j), 1]
+            xt_ref[:, j * BLOCK : (j + 1) * BLOCK] = jnp.transpose(kv_ref[block_of(n, at, j), 0])
         dk_ref[...] = jnp.zeros_like(dk_ref)
         dv_ref[...] = jnp.zeros_like(dv_ref)
 
@@ -528,14 +534,16 @@
                 ds = (p * g).astype(BF)
                 dv += dot(p.astype(BF), gx_ref[rows, :HEAD], NN)
                 dk += dot(ds, qx_ref[rows, :HEAD], NN)
-                dqs_ref[rows, :] += dot(ds, kx_ref[ks, :HEAD], TN)
+                dqs_ref[:, rows] += dot(xt_ref[:, ks], ds, NN)
             dv_ref[ks, :] += dv
             dk_ref[ks, :] += dk
 
         def between():
             @pl.when(s == 7)
             def _():
-                dq_par[...] = (dqs_ref[pl.ds(OWN * UNIT, GIVE * UNIT), :] * scale).astype(BF)
+                dq_par[...] = jnp.transpose(
+                    dqs_ref[:, pl.ds(OWN * UNIT, GIVE * UNIT)] * scale
+                ).astype(BF)
                 dq_home.start()
                 relay(0, 2)
 
@@ -581,7 +589,7 @@
 
     lax.fori_loop(0, 8, backward_group, 0)
     total_first(1)
-    dq_ref[...] = (dqs_ref[pl.ds(0, OWN * UNIT), :] * scale).astype(BF)
+    dq_ref[...] = jnp.transpose(dqs_ref[:, pl.ds(0, OWN * UNIT)] * scale).astype(BF)
     relay(1, 2)
     total_second(0)
 
@@ -653,7 +661,8 @@
             vm((WORK, 2 * HEAD), BF),
             vm((4 * BLOCK, 2 * HEAD), BF),
             vm((4 * BLOCK, 2 * HEAD), BF),
-            vm((WORK, HEAD), F32),
+            vm((HEAD, 4 * BLOCK), BF),
+            vm((HEAD, WORK), F32),
             vm((4 * BLOCK, HEAD), F32),
             vm((4 * BLOCK, HEAD), F32),
             vm((2, 4, 2, 4, BLOCK, HEAD), BF),

time: 138 us -> 137 us (level)
  Pallas kernels: 135 us -> 133 us
    pallas_call x1, Pallas kernels: 133 us -> 131 us  [layer(): pl.pallas_call(functools.partial(layer_kernel, unit, scale), out_shape=(j...]
where the time goes in v3:
time: 137 us; the launch traced here: 134 us
  Pallas kernels  133 us (97%)
    pallas_call x1, Pallas kernels, layer(): pl.pallas_call(functools.partial(layer_kernel, unit, scale), out_shape=(j...  131 us

profile of v3, /device:TPU:0, one launch (start us, length us, event | category | flops | bytes accessed | tf_op | source)
XLA Modules:
  0.0 133.9 jit_solution(792710571809208778)
XLA Ops:
  0.6 130.9 %layer.1 = (bf16[2048,128]{1,0:T(8,128)(2,1)}, bf16[256,128]{1,0:T(8,128)(2,1)}, bf16[256,128]{1,0:T(8,128)(2,1)}, bf16[64,5120]{1,0:T(8,128)(2,1)}) custom-call(bf16[256,128]{1,0:T(8,128)(2,1)} %bitcast.7, bf16[256,128]{1,0:T(8,128)(2,1)} %bitcast.8, bf16[64,5120]{1,0:T(8,128)(2,1)} %cot_ref.1, bf16[2048,128]{1,0:T(8,128)(2,1)} %bitcast.6, ...), custom_call_target="tpu_custom_call" | custom-call | tf_op jit(solution)/shard_map/layer/pallas_call | solution.py:629
  131.6 2.4 %results.1 = (bf16[2048,128]{1,0:T(8,128)(2,1)}, bf16[256,128]{1,0:T(8,128)(2,1)}, bf16[256,128]{1,0:T(8,128)(2,1)}, bf16[64,5120]{1,0:T(8,128)(2,1)}) custom-call(bf16[2048,128]{1,0:T(8,128)(2,1)} %get-tuple-element.12.refs_0_, bf16[256,128]{1,0:T(8,128)(2,1)} %get-tuple-element.13.refs_1_, bf16[256,128]{1,0:T(8,128)(2,1)} %get-tuple-element.14.refs_2_, ...), custom_call_target="tpu_custom_call" | custom-call | tf_op jit(solution)/shard_map/results/pallas_call | solution.py:696

commit v4 on v1

--- a/solution.py
+++ b/solution.py
@@ -26,7 +26,6 @@
 
 NT = (((1,), (1,)), ((), ()))
 NN = (((1,), (0,)), ((), ()))
-TN = (((0,), (0,)), ((), ()))
 
 
 def dot(a, b, dims):
@@ -148,7 +147,7 @@
     dq_ref, gk_ref, gv_ref, o_ref,
     w_ref, wsem, kv_ref, ca_ref, qw_ref, ga_ref, attn_ref, m_row, l_row, acc_ref,
     attn_far, dq_par, dq_far, af_ref, flat_ref, opart, ocore, osum, orow,
-    qx_ref, gx_ref, kx_ref, vx_ref, dqs_ref, dk_ref, dv_ref,
+    qx_ref, gx_ref, kx_ref, vx_ref, xt_ref, dqs_ref, dk_ref, dv_ref,
     p_ref, t_ref, r_ref, m_ref, t2_ref, r2_ref, s_ref, y_ref,
     send, recv, hsend, hrecv,
 ):
@@ -373,13 +372,16 @@
         def _():
             pass_on(1, 2)
             pass_on(1, 3)
+
+        @pl.when(s == 3)
+        def _():
+            pass_on(0, 2)
+            pass_on(0, 3)
+
+        @pl.when(s == 4)
+        def _():
             mail.got("cot row")
             mail.go("cot relay")
-
-        @pl.when(s == 3)
-        def _():
-            pass_on(0, 2)
-            pass_on(0, 3)
 
         @pl.when(s == 5)
         def _():
@@ -392,11 +394,14 @@
                 for step in range(4):
                     mail.got((n_now, "last", step, 0), (n_now, "last", step, 1))
 
+        for j in range(4):
+            xt_ref[:, j * BLOCK : (j + 1) * BLOCK] = jnp.transpose(kv_ref[block_of(n, at, j), 1])
+
         def tile(first, units, j, blocks, ahead):
             rows = rows_of(first, units)
             held = [block_of(n, at, j + i) for i in range(blocks)]
             keys = jnp.concatenate([kv_ref[b, 0] for b in held], axis=0)
-            values = jnp.concatenate([kv_ref[b, 1] for b in held], axis=0)
+            values = xt_ref[:, pl.ds(pl.multiple_of(j * BLOCK, BLOCK), blocks * BLOCK)]
             sc = dot(keys, qw_ref[rows, :], NT)
             if ahead is not None:
                 sc = jnp.where(mask(sc.shape[0], sc.shape[1], ahead), sc, LOW)
@@ -406,7 +411,7 @@
             p = jnp.exp2((sc - new) * unit)
             m_row[:, rows] = new
             l_row[:, rows] = l_row[:, rows] * alpha + jnp.sum(p, axis=0, keepdims=True)
-            acc_ref[:, rows] = acc_ref[:, rows] * alpha + dot(values, p.astype(BF), TN)
+            acc_ref[:, rows] = acc_ref[:, rows] * alpha + dot(values, p.astype(BF), NN)
 
         over_group(n, at, tile)
         return carry
@@ -479,7 +484,7 @@
         delta = jnp.sum(ga.astype(F32) * attn_ref[rows, :].astype(F32), axis=1, keepdims=True)
         gx_ref[rows, :HEAD] = ga
         gx_ref[rows, HEAD:] = tail_of(jnp.broadcast_to(delta, (512, HEAD)))
-        dqs_ref[rows, :] = jnp.zeros((512, HEAD), F32)
+        dqs_ref[:, rows] = jnp.zeros((HEAD, 512), F32)
         return carry
 
     lax.fori_loop(0, WORK // 512, prepare, 0)
@@ -498,6 +503,7 @@
             ks = pl.ds(j * BLOCK, BLOCK)
             kx_ref[ks, :HEAD] = kv_ref[block_of(n, at, j), 0]
             vx_ref[ks, :HEAD] = kv_ref[block_of(n, at, j), 1]
+            xt_ref[:, j * BLOCK : (j + 1) * BLOCK] = jnp.transpose(kv_ref[block_of(n, at, j), 0])
         dk_ref[...] = jnp.zeros_like(dk_ref)
         dv_ref[...] = jnp.zeros_like(dv_ref)
 
@@ -511,12 +517,14 @@
             ds = (p * g).astype(BF)
             dv_ref[ks, :] += dot(p.astype(BF), gx_ref[rows, :HEAD], NN)
             dk_ref[ks, :] += dot(ds, qx_ref[rows, :HEAD], NN)
-            dqs_ref[rows, :] += dot(ds, kx_ref[ks, :HEAD], TN)
+            dqs_ref[:, rows] += dot(xt_ref[:, ks], ds, NN)
 
         def between(own):
             @pl.when(jnp.logical_and(s == 7, own == 0))
             def _():
-                dq_par[...] = (dqs_ref[pl.ds(OWN * UNIT, GIVE * UNIT), :] * scale).astype(BF)
+                dq_par[...] = jnp.transpose(
+                    dqs_ref[:, pl.ds(OWN * UNIT, GIVE * UNIT)] * scale
+                ).astype(BF)
                 dq_home.start()
 
         over_group(n, at, tile, between)
@@ -562,7 +570,7 @@
     lax.fori_loop(0, 8, backward_group, 0)
     total_first(1)
     relay(0, 2)
-    dq_ref[...] = (dqs_ref[pl.ds(0, OWN * UNIT), :] * scale).astype(BF)
+    dq_ref[...] = jnp.transpose(dqs_ref[:, pl.ds(0, OWN * UNIT)] * scale).astype(BF)
     relay(1, 2)
     total_second(0)
 
@@ -633,7 +641,8 @@
             vm((WORK, 2 * HEAD), BF),
             vm((4 * BLOCK, 2 * HEAD), BF),
             vm((4 * BLOCK, 2 * HEAD), BF),
-            vm((WORK, HEAD), F32),
+            vm((HEAD, 4 * BLOCK), BF),
+            vm((HEAD, WORK), F32),
             vm((4 * BLOCK, HEAD), F32),
             vm((4 * BLOCK, HEAD), F32),
             vm((2, 4, 2, 4, BLOCK, HEAD), BF),
@@ -656,6 +665,24 @@
     )(k, v, cot, q, w)
 
 
+def results_kernel(*refs):
+    n = len(refs) // 2
+    for i in range(n):
+        refs[n + i][...] = refs[i][...]
+
+
+def results(*arrays):
+    n = len(arrays)
+    return pl.pallas_call(
+        results_kernel,
+        out_shape=tuple(jax.ShapeDtypeStruct(a.shape, a.dtype) for a in arrays),
+        in_specs=vmem_specs(n),
+        out_specs=tuple(vmem_specs(n)),
+        compiler_params=pltpu.CompilerParams(vmem_limit_bytes=VMEM_LIMIT),
+        name="results",
+    )(*arrays)
+
+
 def vmem_specs(n):
     return [pl.BlockSpec(memory_space=pltpu.VMEM)] * n
 
@@ -664,7 +691,7 @@
     rows, heads, head = queries.shape
     scale = 1.0 / math.sqrt(head)
     unit = scale * math.log2(math.e)
-    grad_queries, grad_keys, grad_values, output = layer(
+    made = layer(
         unit,
         scale,
         key_rows.reshape(rows, head),
@@ -673,6 +700,7 @@
         queries.reshape(rows * heads, head),
         out_weight,
     )
+    grad_queries, grad_keys, grad_values, output = results(*made)
     return (
         output,
         grad_queries.reshape(rows, heads, head),

time: 140 us -> 135 us (0.964)
  local copies, waits for them, and re-layouts: 6.78 us -> 0 us
  Pallas kernels: 132 us -> 135 us
    unnamed x4 -> x0, local copies, waits for them, and re-layouts: 6.78 us -> none
    pallas_call x0 -> x1, Pallas kernels: none -> 2.38 us  [results(): pl.pallas_call(results_kernel, out_shape=tuple((jax.ShapeDtypeStruct(a.sh...]
where the time goes in v4:
time: 135 us
  Pallas kernels  135 us (100%)
    pallas_call x1, Pallas kernels, layer(): pl.pallas_call(functools.partial(layer_kernel, unit, scale), out_shape=(j...  132 us

profile of v4, /device:TPU:98, one launch (start us, length us, event | category | flops | bytes accessed | tf_op | source)
XLA Modules:
  0.0 135.3 jit_solution(10239230842080162425)
XLA Ops:
  0.6 132.3 %layer.1 = (bf16[2048,128]{1,0:T(8,128)(2,1)}, bf16[256,128]{1,0:T(8,128)(2,1)}, bf16[256,128]{1,0:T(8,128)(2,1)}, bf16[64,5120]{1,0:T(8,128)(2,1)}) custom-call(bf16[256,128]{1,0:T(8,128)(2,1)} %bitcast.7, bf16[256,128]{1,0:T(8,128)(2,1)} %bitcast.8, bf16[64,5120]{1,0:T(8,128)(2,1)} %cot_ref.1, bf16[2048,128]{1,0:T(8,128)(2,1)} %bitcast.6, ...), custom_call_target="tpu_custom_call" | custom-call | tf_op jit(solution)/shard_map/layer/pallas_call | solution.py:610
  132.9 2.4 %results.1 = (bf16[2048,128]{1,0:T(8,128)(2,1)}, bf16[256,128]{1,0:T(8,128)(2,1)}, bf16[256,128]{1,0:T(8,128)(2,1)}, bf16[64,5120]{1,0:T(8,128)(2,1)}) custom-call(bf16[2048,128]{1,0:T(8,128)(2,1)} %get-tuple-element.12.refs_0_, bf16[256,128]{1,0:T(8,128)(2,1)} %get-tuple-element.13.refs_1_, bf16[256,128]{1,0:T(8,128)(2,1)} %get-tuple-element.14.refs_2_, ...), custom_call_target="tpu_custom_call" | custom-call | tf_op jit(solution)/shard_map/results/pallas_call | solution.py:676

commit v5 on v2

--- a/solution.py
+++ b/solution.py
@@ -22,6 +22,8 @@
 GIVE = 4
 WORK = (OWN + GIVE) * UNIT
 LOW = -1e30
+WIDE = 1024
+SLOTS = 146
 VMEM_LIMIT = 60 * 1024 * 1024
 
 NT = (((1,), (1,)), ((), ()))
@@ -37,7 +39,7 @@
     c = lax.axis_index("ctx")
     low = jnp.minimum(c, NCTX - 1 - c)
     given = jnp.where(
-        low <= 2, 4, jnp.where(low <= 8, 3, jnp.where(low <= 11, 2, jnp.where(low <= 14, 1, 0)))
+        low <= 2, 4, jnp.where(low <= 7, 3, jnp.where(low <= 11, 2, jnp.where(low <= 14, 1, 0)))
     )
     return c, c < NCTX // 2, given
 
@@ -49,6 +51,14 @@
 
 def ctx_of(y, z, x):
     return (y * ZS + z) * XS + x
+
+
+def turned_back(own, i):
+    return (own + jnp.where(i == 0, 0, jnp.where(i == 1, 1, jnp.where(i == 2, 3, 2)))) % 4
+
+
+def turned(own, i):
+    return (own + jnp.where(i == 0, 2, jnp.where(i == 1, 1, jnp.where(i == 2, 3, 0)))) % 4
 
 
 def neighbours():
@@ -69,10 +79,11 @@
 
 class Courier:
     def __init__(self, send, recv):
-        self.send, self.recv, self.made = send, recv, {}
+        self.send, self.recv, self.made, self.count = send, recv, {}, 0
 
     def plan(self, name, axis, other, src, dst):
-        n = len(self.made)
+        n = self.count
+        self.count += 1
         self.made[name] = lambda: pltpu.make_async_remote_copy(
             src_ref=src,
             dst_ref=dst,
@@ -90,9 +101,12 @@
         for name in names:
             self.made[name]().wait_recv()
 
+    def sent(self, *names):
+        for name in names:
+            self.made.pop(name)().wait_send()
+
     def finish(self):
-        for copy in self.made.values():
-            copy().wait_send()
+        self.sent(*list(self.made))
 
 
 class Handover:
@@ -131,24 +145,13 @@
         self.each(self.sends, lambda i: self.copy(i).wait_send())
 
 
-def tail_of(x):
-    one = x.astype(BF).astype(F32)
-    rest = x - one
-    two = rest.astype(BF).astype(F32)
-    three = rest - two
-    lane = lax.broadcasted_iota(jnp.int32, x.shape, 1)
-    return jnp.where(
-        lane == 0, -one, jnp.where(lane == 1, -two, jnp.where(lane == 2, -three, 0.0))
-    ).astype(BF)
-
-
 def layer_kernel(
     unit, scale,
     k_ref, v_ref, cot_ref, q_ref, w_hbm,
     dq_ref, gk_ref, gv_ref, o_ref,
-    w_ref, wsem, kv_ref, ca_ref, gt_ref, qw_ref, ga_ref, attn_ref, m_row, l_row, acc_ref,
-    attn_far, dq_par, dq_far, af_ref, flat_ref, opart, ocore, osum, orow,
-    qx_ref, gx_ref, kx_ref, vx_ref, dqs_ref, dk_ref, dv_ref,
+    w_ref, wsem, kv_ref, ca_ref, gt_ref, qw_ref, ga_ref, attn_ref, kept_ref, top_ref, m_row, l_row, acc_ref,
+    attn_far, dq_par, dq_far, af_ref, flat_ref, ocore, osum, orow,
+    dqs_ref, dk_ref, dv_ref,
     p_ref, t_ref, r_ref, m_ref, t2_ref, r2_ref, s_ref, y_ref,
     send, recv, hsend, hrecv,
 ):
@@ -158,8 +161,28 @@
     core, row = h ^ 1, h ^ 2
     mine, up = h % 2, h // 2
     partner, xs, zs = neighbours()
-    w_copy = pltpu.make_async_copy(w_hbm, w_ref, wsem)
-    w_copy.start()
+
+    def w_copy(i):
+        cols = pl.ds(pl.multiple_of(i * WIDE, WIDE), WIDE)
+        return pltpu.make_async_copy(w_hbm.at[:, cols], w_ref.at[i % 2], wsem.at[i % 2])
+
+    def over_weight(act):
+        chunks = w_hbm.shape[1] // WIDE
+
+        def chunk(i, carry):
+            w_copy(i).wait()
+            act(i, w_ref.at[i % 2])
+
+            @pl.when(i + 2 < chunks)
+            def _():
+                w_copy(i + 2).start()
+
+            return carry
+
+        lax.fori_loop(0, chunks, chunk, 0)
+
+    w_copy(0).start()
+    w_copy(1).start()
     greet([partner] + xs + zs + [NCTX - 1 - c], [core, row])
     mail = Courier(send, recv)
 
@@ -174,7 +197,6 @@
     gs = hand(1, ga_ref, 0, ga_ref, OWN, False)
     attn_home = hand(2, attn_ref, OWN, attn_far, 0, True)
     dq_home = hand(3, dq_par, 0, dq_far, 0, True)
-    qs.start()
     ca_ref[h] = cot_ref[...]
     for name, o, i in (("cot row", row, h), ("cot core", core, h), ("cot relay", core, row)):
         mail.plan(name, "head", o, ca_ref.at[i], ca_ref.at[i])
@@ -215,7 +237,7 @@
                 mail.plan((n, stage, "sum", d), "ctx", to[d], t.at[d], r.at[d, d])
     mail.plan("y", "ctx", partner, s_ref.at[y], y_ref)
     for i in range(2):
-        mail.plan(("core", i), "head", core, opart.at[2 * i + 1 - mine], ocore.at[i])
+        mail.plan(("core", i), "head", core, ca_ref.at[2 * i + 1 - mine], ocore.at[i])
     mail.plan("row", "head", row, osum.at[1 - up], orow)
 
     def far(n, stage):
@@ -224,35 +246,31 @@
     def near(n, stage, d):
         mail.go((n, stage, "near", d))
 
-    def relay(n, stage):
+    def relay(n, stage, d):
         piece, at, t = (
             (p_ref.at[n], (x, z)[n], t_ref.at[n])
             if stage == 1
             else (m_ref.at[n], (z, x)[n], t2_ref.at[n])
         )
-        for d in range(2):
-            nxt = (at + (1, 3)[d]) % 4
-            mail.got((n, stage, "far", d))
-            t[d] = (piece[nxt, d].astype(F32) + t[d].astype(F32)).astype(BF)
-            mail.go((n, stage, "sum", d))
+        nxt = (at + (1, 3)[d]) % 4
+        mail.got((n, stage, "far", d))
+        t[d] = (piece[nxt, d].astype(F32) + t[d].astype(F32)).astype(BF)
+        mail.go((n, stage, "sum", d))
 
     def arrived(n, stage):
         for d in range(2):
             mail.got((n, stage, "near", d), (n, stage, "sum", d))
 
-    def total_first(n):
-        arrived(n, 1)
+    def total_first(n, places):
         at = (x, z)[n]
-        for kv in range(2):
-            for j in range(4):
+        for place_now in places:
+            j = turned((z, x)[n], place_now)
+            for kv in range(2):
                 m_ref[n, j, kv] = (
                     p_ref[n, at, kv, j].astype(F32)
                     + r_ref[n, 0, kv, j].astype(F32)
                     + r_ref[n, 1, kv, j].astype(F32)
                 ).astype(BF)
-        far(n, 2)
-        near(n, 2, 0)
-        near(n, 2, 1)
 
     def total_second(n):
         arrived(n, 2)
@@ -275,66 +293,76 @@
             flat_ref[:, i * HEAD : (i + 1) * HEAD] = af_ref[
                 pl.ds(i, BLOCK, stride=GROUP), :
             ].astype(BF)
-        wide = 512
-
-        def chunk(n, carry):
-            cols = pl.ds(pl.multiple_of(n * wide, wide), wide)
-            part = dot(flat_ref[...], w_ref[:, cols], NN).astype(BF)
-            opart[:, :, cols] = part.reshape(4, BLOCK // 4, wide)
-            return carry
-
-        lax.fori_loop(0, w_ref.shape[1] // wide, chunk, 0)
+        mail.sent("cot row", "cot core", "cot relay")
+
+        def project(i, w):
+            cols = pl.ds(pl.multiple_of(i * WIDE, WIDE), WIDE)
+            part = dot(flat_ref[...], w[...], NN).astype(BF)
+            ca_ref[:, :, cols] = part.reshape(4, BLOCK // 4, WIDE)
+
+        over_weight(project)
         mail.go(("core", 0), ("core", 1))
 
     def output_core():
         for i in range(2):
             mail.got(("core", i))
-            osum[i] = (opart[2 * i + mine].astype(F32) + ocore[i].astype(F32)).astype(BF)
+            osum[i] = (ca_ref[2 * i + mine].astype(F32) + ocore[i].astype(F32)).astype(BF)
         mail.go("row")
 
     begin = jnp.where(is_low, 0, given)
     taken = OWN + jnp.where(is_low, given, 0)
 
-    def block_of(n, at, j):
+    def inner(n, i):
+        return turned(jnp.where(n == 0, z, x), i)
+
+    def block_of(n, at, i, own_first=False):
+        j = turned_back(jnp.where(n == 0, z, x), i) if own_first else inner(n, i)
         return jnp.where(n == 0, 16 + 4 * j + at, 4 * at + j)
 
-    def over_group(n, at, tile, own_first, between):
+    def over_pair(n, at, jp, tile, own_first, between, turns=(0, 2)):
+        last = jnp.maximum(
+            block_of(n, at, 2 * jp, own_first), block_of(n, at, 2 * jp + 1, own_first)
+        )
+
         def row_set(turn, carry):
             mine_now = turn == (0 if own_first else 1)
             u0 = jnp.where(mine_now, begin, OWN)
             u1 = jnp.where(mine_now, OWN, taken)
             qb = jnp.where(mine_now, c, NCTX - 1 - c)
             pos0 = jnp.where(mine_now, 0, OWN)
-            count = u1 - u0
-
-            def key_pair(jp, carry):
-                whole = qb > block_of(n, at, 2 * jp + 1)
-
-                def rows(on, j, blocks, ahead):
-                    def many(i, carry):
-                        tile(u0 + 4 * i, (2, 2), j, blocks, ahead, u0 + 4 * i - pos0)
-                        return carry
-
-                    lax.fori_loop(0, jnp.where(on, count // 4, 0), many, 0)
-                    rest = jnp.where(on, count % 4, 0)
-                    for k, chains in ((3, (2, 1)), (2, (1, 1)), (1, (1,))):
-
-                        @pl.when(rest == k)
-                        def _():
-                            tile(u1 - k, chains, j, blocks, ahead, u1 - k - pos0)
-
-                rows(whole, 2 * jp, 2, None)
-
-                def single_block(j, carry):
-                    ahead = (qb - block_of(n, at, j)) * BLOCK
-                    some = jnp.logical_and(jnp.logical_not(whole), ahead >= 0)
-                    rows(some, j, 1, ahead)
+            twos = (u1 - u0) // 2
+            odd = (u1 - u0) % 2
+            whole = qb > last
+
+            def full(i, carry):
+                tile(u0 + 2 * i, 2, 2 * jp, 2, None)
+                return carry
+
+            lax.fori_loop(0, jnp.where(whole, twos, 0), full, 0)
+
+            @pl.when(jnp.logical_and(whole, odd == 1))
+            def _():
+                tile(u1 - 1, 1, 2 * jp, 2, None)
+
+            def single_block(j, carry):
+                ahead = (qb - block_of(n, at, j, own_first)) * BLOCK
+                some = jnp.logical_and(jnp.logical_not(whole), ahead >= 0)
+
+                def part(i, carry):
+                    u = u0 + 2 * i
+                    tile(u, 2, j, 1, ahead + (u - pos0) * UNIT_POS)
                     return carry
 
-                lax.fori_loop(2 * jp, 2 * jp + 2, single_block, 0)
+                lax.fori_loop(0, jnp.where(some, twos, 0), part, 0)
+
+                @pl.when(jnp.logical_and(some, odd == 1))
+                def _():
+                    u = u1 - 1
+                    tile(u, 1, j, 1, ahead + (u - pos0) * UNIT_POS)
+
                 return carry
 
-            lax.fori_loop(0, 2, key_pair, 0)
+            lax.fori_loop(2 * jp, 2 * jp + 2, single_block, 0)
 
             @pl.when(turn == 0)
             def _():
@@ -342,7 +370,21 @@
 
             return carry
 
-        lax.fori_loop(0, 2, row_set, 0)
+        lax.fori_loop(turns[0], turns[1], row_set, 0)
+
+    def slot_of(b, u):
+        own = b * (OWN - begin) + u - begin
+        far = (c + 1) * (OWN - begin) + b * (taken - OWN) + u - OWN
+        return jnp.where(u < OWN, own, far)
+
+    def parts(first, units, held):
+        for k, b in enumerate(held):
+            for i in range(units):
+                yield (
+                    slot_of(b, first + i),
+                    slice(k * BLOCK, (k + 1) * BLOCK),
+                    slice(i * UNIT, (i + 1) * UNIT),
+                )
 
     def rows_of(first, units):
         return pl.ds(pl.multiple_of(first * UNIT, UNIT), units * UNIT)
@@ -353,28 +395,29 @@
 
     def forward_group(s, carry):
         n = (1 - y + s) % 2
-        i = s // 2
+        i = s % 8 // 2
         off = jnp.where(i == 0, 0, jnp.where(i == 1, 3, jnp.where(i == 2, 1, 2)))
         at = (jnp.where(n == 0, x, z) + off) % 4
 
         @pl.when(s == 1)
         def _():
+            each_pass(False, front_end)
             each_pass(True, lambda n: (pass_on(n, 0), pass_on(n, 1)))
 
         @pl.when(s == 2)
         def _():
             each_pass(True, lambda n: (pass_on(n, 2), pass_on(n, 3)))
             each_pass(False, lambda n: (pass_on(n, 0), pass_on(n, 1)))
+            qs.wait_recv()
+
+        @pl.when(s == 3)
+        def _():
+            each_pass(False, lambda n: (pass_on(n, 2), pass_on(n, 3)))
+
+        @pl.when(s == 5)
+        def _():
             mail.got("cot row")
             mail.go("cot relay")
-
-        @pl.when(s == 3)
-        def _():
-            each_pass(False, lambda n: (pass_on(n, 2), pass_on(n, 3)))
-
-        @pl.when(s == 5)
-        def _():
-            project_cotangent()
 
         def arrived_last(n):
             for step in range(4):
@@ -382,52 +425,59 @@
 
         @pl.when(s == 6)
         def _():
+            project_cotangent()
             each_pass(True, arrived_last)
 
         @pl.when(s == 7)
         def _():
             each_pass(False, arrived_last)
 
-        def tile(first, chains, j, blocks, ahead, unit_at):
-            held = [block_of(n, at, j + i) for i in range(blocks)]
+        def tile(first, units, j, blocks, ahead):
+            rows = rows_of(first, units)
+            held = [block_of(n, at, j + i, True) for i in range(blocks)]
             keys = jnp.concatenate([kv_ref[b, 0] for b in held], axis=0)
             values = jnp.concatenate([kv_ref[b, 1] for b in held], axis=0)
-            offsets = [sum(chains[:i]) for i in range(len(chains))]
-            sets = [rows_of(first + o, units) for o, units in zip(offsets, chains)]
-            scores = [dot(keys, qw_ref[rows, :], NT) for rows in sets]
-            for rows, o, sc in zip(sets, offsets, scores):
-                if ahead is not None:
-                    past = ahead + (unit_at + o) * UNIT_POS
-                    sc = jnp.where(mask(sc.shape[0], sc.shape[1], past), sc, LOW)
-                top = m_row[:, rows]
-                new = jnp.maximum(top, jnp.max(sc, axis=0, keepdims=True))
-                alpha = jnp.exp2((top - new) * unit)
-                p = jnp.exp2((sc - new) * unit)
-                m_row[:, rows] = new
-                l_row[:, rows] = l_row[:, rows] * alpha + jnp.sum(p, axis=0, keepdims=True)
-                acc_ref[:, rows] = acc_ref[:, rows] * alpha + dot(values, p.astype(BF), TN)
-
-        def between():
-            @pl.when(s == 0)
+            sc = dot(keys, qw_ref[rows, :], NT)
+            if ahead is not None:
+                sc = jnp.where(mask(sc.shape[0], sc.shape[1], ahead), sc, LOW)
+            top = m_row[:, rows]
+            new = jnp.maximum(top, jnp.max(sc, axis=0, keepdims=True))
+            alpha = jnp.exp2((top - new) * unit)
+            p = jnp.exp2((sc - new) * unit)
+            m_row[:, rows] = new
+            l_row[:, rows] = l_row[:, rows] * alpha + jnp.sum(p, axis=0, keepdims=True)
+            p = p.astype(BF)
+            acc_ref[:, rows] = acc_ref[:, rows] * alpha + dot(values, p, TN)
+            for slot, ks, us in parts(first, units, held):
+                kept_ref[slot] = p[ks, us]
+                top_ref[slot] = new[:, us]
+
+        def pair(jp, carry):
+            turns = (jnp.where(s >= 8, 1, 0), jnp.where(s < 2, 1, 2))
+            over_pair(n, at, jp, tile, True, lambda: None, turns)
+
+            @pl.when(jnp.logical_and(s == 0, jp == 0))
             def _():
-                qs.wait_recv()
-
-        over_group(n, at, tile, True, between)
+                each_pass(True, front_end)
+                each_pass(False, front)
+                mail.go("cot row", "cot core")
+
+            return carry
+
+        lax.fori_loop(0, 2, pair, 0)
         return carry
 
     def project_cotangent():
         mail.got("cot core", "cot relay")
-        w_copy.wait()
-
-        wide = 1024
         gt_ref[...] = jnp.zeros_like(gt_ref)
 
-        def project(n, carry):
-            cols = pl.ds(pl.multiple_of(n * wide, wide), wide)
-            gt_ref[...] += dot(w_ref[:, cols], ca_ref[:, :, cols].reshape(BLOCK, wide), NT)
-            return carry
-
-        lax.fori_loop(0, w_ref.shape[1] // wide, project, 0)
+        def project(i, w):
+            cols = pl.ds(pl.multiple_of(i * WIDE, WIDE), WIDE)
+            gt_ref[...] += dot(w[...], ca_ref[:, :, cols].reshape(BLOCK, WIDE), NT)
+
+        over_weight(project)
+        w_copy(0).start()
+        w_copy(1).start()
         for i in range(GROUP):
             af_ref[pl.ds(i, BLOCK, stride=GROUP), :] = jnp.transpose(
                 gt_ref[i * HEAD : (i + 1) * HEAD, :]
@@ -449,6 +499,8 @@
         for d in range(2):
             mail.got((n, "beside", d))
             mail.go((n, "on", d), (n, "third", 1 + d, 0), (n, "third", 1 + d, 1))
+
+    def front_end(n):
         mail.got((n, "on", 0), (n, "on", 1))
         mail.go((n, "third", 3, 0), (n, "third", 3, 1))
 
@@ -459,26 +511,15 @@
     acc_ref[...] = jnp.zeros_like(acc_ref)
     mail.got("pair")
     each_pass(False, start)
-    mail.go("cot row", "cot core")
+    qs.start()
     each_pass(True, front)
-    each_pass(False, front)
-    lax.fori_loop(0, 8, forward_group, 0)
+    lax.fori_loop(0, 10, forward_group, 0)
 
     def finish_forward(i, carry):
         rows = pl.ds(pl.multiple_of(i * 512, 512), 512)
         l = l_row[:, rows]
         attn_ref[rows, :] = jnp.transpose(acc_ref[:, rows] / l).astype(BF)
-        lse = m_row[:, rows] + jnp.log2(l) / unit
-        one = lse.astype(BF).astype(F32)
-        rest = lse - one
-        two = rest.astype(BF).astype(F32)
-        three = rest - two
-        which = lax.broadcasted_iota(jnp.int32, (HEAD, 512), 0)
-        pieces = jnp.where(
-            which == 0, -one, jnp.where(which == 1, -two, jnp.where(which == 2, -three, 0.0))
-        )
-        qx_ref[rows, :HEAD] = qw_ref[rows, :]
-        qx_ref[rows, HEAD:] = jnp.transpose(pieces).astype(BF)
+        m_row[:, rows] = m_row[:, rows] * unit + jnp.log2(l)
         return carry
 
     lax.fori_loop(0, WORK // 512, finish_forward, 0)
@@ -487,18 +528,12 @@
 
     def prepare(i, carry):
         rows = pl.ds(pl.multiple_of(i * 512, 512), 512)
-        ga = ga_ref[rows, :]
-        delta = jnp.sum(ga.astype(F32) * attn_ref[rows, :].astype(F32), axis=1, keepdims=True)
-        gx_ref[rows, :HEAD] = ga
-        gx_ref[rows, HEAD:] = tail_of(jnp.broadcast_to(delta, (512, HEAD)))
+        products = ga_ref[rows, :].astype(F32) * attn_ref[rows, :].astype(F32)
+        l_row[:, rows] = jnp.sum(jnp.transpose(products), axis=0, keepdims=True)
         dqs_ref[rows, :] = jnp.zeros((512, HEAD), F32)
         return carry
 
     lax.fori_loop(0, WORK // 512, prepare, 0)
-    lane = lax.broadcasted_iota(jnp.int32, (4 * BLOCK, HEAD), 1)
-    ones = jnp.where(lane < 3, 1.0, 0.0).astype(BF)
-    kx_ref[:, HEAD:] = ones
-    vx_ref[:, HEAD:] = ones
 
     def backward_group(s, carry):
         n = s % 2
@@ -506,44 +541,61 @@
         off = jnp.where(i == 0, 2, jnp.where(i == 1, 1, jnp.where(i == 2, 3, 0)))
         at = (jnp.where(n == 0, x, z) + off) % 4
 
-        for j in range(4):
-            ks = pl.ds(j * BLOCK, BLOCK)
-            kx_ref[ks, :HEAD] = kv_ref[block_of(n, at, j), 0]
-            vx_ref[ks, :HEAD] = kv_ref[block_of(n, at, j), 1]
-        dk_ref[...] = jnp.zeros_like(dk_ref)
-        dv_ref[...] = jnp.zeros_like(dv_ref)
-
-        def tile(first, chains, j, blocks, ahead, unit_at):
-            ks = pl.ds(pl.multiple_of(j * BLOCK, BLOCK), blocks * BLOCK)
-            offsets = [sum(chains[:i]) for i in range(len(chains))]
-            sets = [rows_of(first + o, units) for o, units in zip(offsets, chains)]
-            scores = [dot(kx_ref[ks, :], qx_ref[rows, :], NT) for rows in sets]
-            grads = [dot(vx_ref[ks, :], gx_ref[rows, :], NT) for rows in sets]
-            dv, dk = 0.0, 0.0
-            for rows, o, sc, g in zip(sets, offsets, scores, grads):
-                p = jnp.exp2(sc * unit)
-                if ahead is not None:
-                    past = ahead + (unit_at + o) * UNIT_POS
-                    p = jnp.where(mask(p.shape[0], p.shape[1], past), p, 0.0)
-                ds = (p * g).astype(BF)
-                dv += dot(p.astype(BF), gx_ref[rows, :HEAD], NN)
-                dk += dot(ds, qx_ref[rows, :HEAD], NN)
-                dqs_ref[rows, :] += dot(ds, kx_ref[ks, :HEAD], TN)
-            dv_ref[ks, :] += dv
-            dk_ref[ks, :] += dk
-
-        def between():
-            @pl.when(s == 7)
+        def tile(first, units, j, blocks, ahead):
+            rows = rows_of(first, units)
+            held = [block_of(n, at, j + i) for i in range(blocks)]
+            keys = jnp.concatenate([kv_ref[b, 0] for b in held], axis=0)
+            values = jnp.concatenate([kv_ref[b, 1] for b in held], axis=0)
+            q = qw_ref[rows, :]
+            ga = ga_ref[rows, :]
+            lse = m_row[:, rows]
+            pieces = [
+                kept_ref[slot].astype(F32) * jnp.exp2(top_ref[slot] * unit - lse[:, us])
+                for slot, ks, us in parts(first, units, held)
+            ]
+            p = jnp.concatenate(
+                [
+                    jnp.concatenate(pieces[k * units : (k + 1) * units], axis=1)
+                    for k in range(blocks)
+                ],
+                axis=0,
+            )
+            ds = (p * (dot(values, ga, NT) - l_row[:, rows])).astype(BF)
+            ks = pl.ds(pl.multiple_of(j % 2 * BLOCK, BLOCK), blocks * BLOCK)
+            dv_ref[ks, :] += dot(p.astype(BF), ga, NN)
+            dk_ref[ks, :] += dot(ds, q, NN)
+            dqs_ref[rows, :] += dot(ds, keys, TN)
+
+        def pair(jp, carry):
+            dk_ref[...] = jnp.zeros_like(dk_ref)
+            dv_ref[...] = jnp.zeros_like(dv_ref)
+
+            def between():
+                @pl.when(jnp.logical_and(s == 7, jp == 1))
+                def _():
+                    far_rows = pl.ds(OWN * UNIT, GIVE * UNIT)
+                    dq_par[...] = (dqs_ref[far_rows, :] * scale).astype(BF)
+                    dq_home.start()
+                    relay(0, 2, 0)
+                    relay(0, 2, 1)
+
+            over_pair(n, at, jp, tile, False, between)
+            for i in range(2):
+                ks = pl.ds(i * BLOCK, BLOCK)
+                j = inner(n, 2 * jp + i)
+                p_ref[n, at, 0, j] = (dk_ref[ks, :] * scale).astype(BF)
+                p_ref[n, at, 1, j] = dv_ref[ks, :].astype(BF)
+
+            @pl.when(jnp.logical_and(s == 7, jp == 0))
             def _():
-                dq_par[...] = (dqs_ref[pl.ds(OWN * UNIT, GIVE * UNIT), :] * scale).astype(BF)
-                dq_home.start()
-                relay(0, 2)
-
-        over_group(n, at, tile, False, between)
-        for j in range(4):
-            ks = pl.ds(j * BLOCK, BLOCK)
-            p_ref[n, at, 0, j] = (dk_ref[ks, :] * scale).astype(BF)
-            p_ref[n, at, 1, j] = dv_ref[ks, :].astype(BF)
+                arrived(1, 1)
+                total_first(1, (0, 1))
+                far(1, 2)
+                near(1, 2, 0)
+
+            return carry
+
+        lax.fori_loop(0, 2, pair, 0)
 
         @pl.when(s == 0)
         def _():
@@ -556,33 +608,41 @@
         @pl.when(s == 2)
         def _():
             near(0, 1, 0)
+            relay(0, 1, 0)
             output_projection()
 
         @pl.when(s == 3)
         def _():
             near(1, 1, 0)
+            relay(1, 1, 0)
 
         @pl.when(s == 4)
         def _():
             near(0, 1, 1)
-            relay(0, 1)
+            relay(0, 1, 1)
             output_core()
 
         @pl.when(s == 5)
         def _():
             near(1, 1, 1)
-            relay(1, 1)
+            relay(1, 1, 1)
 
         @pl.when(s == 6)
         def _():
-            total_first(0)
+            arrived(0, 1)
+            total_first(0, range(4))
+            far(0, 2)
+            near(0, 2, 0)
+            near(0, 2, 1)
 
         return carry
 
     lax.fori_loop(0, 8, backward_group, 0)
-    total_first(1)
+    total_first(1, (2, 3))
+    near(1, 2, 1)
     dq_ref[...] = (dqs_ref[pl.ds(0, OWN * UNIT), :] * scale).astype(BF)
-    relay(1, 2)
+    relay(1, 2, 0)
+    relay(1, 2, 1)
     total_second(0)
 
     @pl.when(y == 0)
@@ -629,14 +689,16 @@
         in_specs=vmem_specs(4) + [pl.BlockSpec(memory_space=pl.ANY)],
         out_specs=tuple(vmem_specs(4)),
         scratch_shapes=[
-            vm(w.shape, BF),
-            dma,
+            vm((2, w.shape[0], WIDE), BF),
+            dma((2,)),
             vm((NCTX, 2, BLOCK, HEAD), BF),
             vm((4,) + cot.shape, BF),
             vm((GROUP * HEAD, BLOCK), F32),
             vm((WORK, HEAD), BF),
             vm((WORK, HEAD), BF),
             vm((WORK, HEAD), BF),
+            vm((SLOTS, BLOCK, UNIT), BF),
+            vm((SLOTS, 1, UNIT), F32),
             vm((1, WORK), F32),
             vm((1, WORK), F32),
             vm((HEAD, WORK), F32),
@@ -645,17 +707,12 @@
             vm((GIVE * UNIT, HEAD), BF),
             vm((OWN * UNIT, HEAD), F32),
             vm((BLOCK, GROUP * HEAD), BF),
-            vm((4,) + part, BF),
             vm((2,) + part, BF),
             vm((2,) + part, BF),
             vm(part, BF),
-            vm((WORK, 2 * HEAD), BF),
-            vm((WORK, 2 * HEAD), BF),
-            vm((4 * BLOCK, 2 * HEAD), BF),
-            vm((4 * BLOCK, 2 * HEAD), BF),
             vm((WORK, HEAD), F32),
-            vm((4 * BLOCK, HEAD), F32),
-            vm((4 * BLOCK, HEAD), F32),
+            vm((2 * BLOCK, HEAD), F32),
+            vm((2 * BLOCK, HEAD), F32),
             vm((2, 4, 2, 4, BLOCK, HEAD), BF),
             vm((2, 2, 4, BLOCK, HEAD), BF),
             vm((2, 2, 2, 4, BLOCK, HEAD), BF),

time: 138 us -> 134 us (0.971); the launches traced: 136 us -> 134 us
  Pallas kernels: 135 us -> 133 us
    pallas_call x1, Pallas kernels: 133 us -> 131 us  [layer(): pl.pallas_call(functools.partial(layer_kernel, unit, scale), out_shape=(j...]
where the time goes in v5:
time: 134 us
  Pallas kernels  133 us (99%)
    pallas_call x1, Pallas kernels, layer(): pl.pallas_call(functools.partial(layer_kernel, unit, scale), out_shape=(j...  131 us

profile of v5, /device:TPU:0, one launch (start us, length us, event | category | flops | bytes accessed | tf_op | source)
XLA Modules:
  0.0 133.5 jit_solution(1934270267871406339)
XLA Ops:
  0.6 130.5 %layer.1 = (bf16[2048,128]{1,0:T(8,128)(2,1)}, bf16[256,128]{1,0:T(8,128)(2,1)}, bf16[256,128]{1,0:T(8,128)(2,1)}, bf16[64,5120]{1,0:T(8,128)(2,1)}) custom-call(bf16[256,128]{1,0:T(8,128)(2,1)} %bitcast.7, bf16[256,128]{1,0:T(8,128)(2,1)} %bitcast.8, bf16[64,5120]{1,0:T(8,128)(2,1)} %cot_ref.1, bf16[2048,128]{1,0:T(8,128)(2,1)} %bitcast.6, ...), custom_call_target="tpu_custom_call" | custom-call | tf_op jit(solution)/shard_map/layer/pallas_call | solution.py:681
  131.2 2.4 %results.1 = (bf16[2048,128]{1,0:T(8,128)(2,1)}, bf16[256,128]{1,0:T(8,128)(2,1)}, bf16[256,128]{1,0:T(8,128)(2,1)}, bf16[64,5120]{1,0:T(8,128)(2,1)}) custom-call(bf16[2048,128]{1,0:T(8,128)(2,1)} %get-tuple-element.12.refs_0_, bf16[256,128]{1,0:T(8,128)(2,1)} %get-tuple-element.13.refs_1_, bf16[256,128]{1,0:T(8,128)(2,1)} %get-tuple-element.14.refs_2_, ...), custom_call_target="tpu_custom_call" | custom-call | tf_op jit(solution)/shard_map/results/pallas_call | solution.py:744

commit v6 on v5

--- a/solution.py
+++ b/solution.py
@@ -22,6 +22,7 @@
 GIVE = 4
 WORK = (OWN + GIVE) * UNIT
 LOW = -1e30
+CUT = (0, 3, 5)
 WIDE = 1024
 SLOTS = 146
 VMEM_LIMIT = 60 * 1024 * 1024
@@ -166,7 +167,7 @@
         cols = pl.ds(pl.multiple_of(i * WIDE, WIDE), WIDE)
         return pltpu.make_async_copy(w_hbm.at[:, cols], w_ref.at[i % 2], wsem.at[i % 2])
 
-    def over_weight(act):
+    def over_weight(act, first, last):
         chunks = w_hbm.shape[1] // WIDE
 
         def chunk(i, carry):
@@ -179,7 +180,7 @@
 
             return carry
 
-        lax.fori_loop(0, chunks, chunk, 0)
+        lax.fori_loop(first, last, chunk, 0)
 
     w_copy(0).start()
     w_copy(1).start()
@@ -236,9 +237,12 @@
                 )
                 mail.plan((n, stage, "sum", d), "ctx", to[d], t.at[d], r.at[d, d])
     mail.plan("y", "ctx", partner, s_ref.at[y], y_ref)
-    for i in range(2):
-        mail.plan(("core", i), "head", core, ca_ref.at[2 * i + 1 - mine], ocore.at[i])
-    mail.plan("row", "head", row, osum.at[1 - up], orow)
+    part_cols = [pl.ds(CUT[k] * WIDE, (CUT[k + 1] - CUT[k]) * WIDE) for k in range(2)]
+    for k, cols in enumerate(part_cols):
+        for i in range(2):
+            src = ca_ref.at[2 * i + 1 - mine, :, cols]
+            mail.plan(("core", k, i), "head", core, src, ocore.at[i, :, cols])
+        mail.plan(("row", k), "head", row, osum.at[1 - up, :, cols], orow.at[:, cols])
 
     def far(n, stage):
         mail.go((n, stage, "far", 0), (n, stage, "far", 1))
@@ -279,35 +283,39 @@
             m_ref[n, at].astype(F32) + r2_ref[n, 0].astype(F32) + r2_ref[n, 1].astype(F32)
         ).astype(BF)
 
-    def output_projection():
-        attn_home.wait_recv()
-        own = OWN * UNIT
-        af_ref[...] = attn_ref[pl.ds(0, own), :].astype(F32)
-
-        def place_far(i):
-            rows = pl.ds(i * UNIT, UNIT)
-            af_ref[rows, :] = attn_far[rows, :].astype(F32)
-
-        attn_home.each(attn_home.takes, place_far)
-        for i in range(GROUP):
-            flat_ref[:, i * HEAD : (i + 1) * HEAD] = af_ref[
-                pl.ds(i, BLOCK, stride=GROUP), :
-            ].astype(BF)
-        mail.sent("cot row", "cot core", "cot relay")
+    def output_projection(k):
+        if k == 0:
+            attn_home.wait_recv()
+            own = OWN * UNIT
+            af_ref[...] = attn_ref[pl.ds(0, own), :].astype(F32)
+
+            def place_far(i):
+                rows = pl.ds(i * UNIT, UNIT)
+                af_ref[rows, :] = attn_far[rows, :].astype(F32)
+
+            attn_home.each(attn_home.takes, place_far)
+            for i in range(GROUP):
+                flat_ref[:, i * HEAD : (i + 1) * HEAD] = af_ref[
+                    pl.ds(i, BLOCK, stride=GROUP), :
+                ].astype(BF)
+            mail.sent("cot row", "cot core", "cot relay")
 
         def project(i, w):
             cols = pl.ds(pl.multiple_of(i * WIDE, WIDE), WIDE)
             part = dot(flat_ref[...], w[...], NN).astype(BF)
             ca_ref[:, :, cols] = part.reshape(4, BLOCK // 4, WIDE)
 
-        over_weight(project)
-        mail.go(("core", 0), ("core", 1))
-
-    def output_core():
+        over_weight(project, CUT[k], CUT[k + 1])
+        mail.go(("core", k, 0), ("core", k, 1))
+
+    def output_core(k):
+        cols = part_cols[k]
         for i in range(2):
-            mail.got(("core", i))
-            osum[i] = (ca_ref[2 * i + mine].astype(F32) + ocore[i].astype(F32)).astype(BF)
-        mail.go("row")
+            mail.got(("core", k, i))
+            osum[i, :, cols] = (
+                ca_ref[2 * i + mine, :, cols].astype(F32) + ocore[i, :, cols].astype(F32)
+            ).astype(BF)
+        mail.go(("row", k))
 
     begin = jnp.where(is_low, 0, given)
     taken = OWN + jnp.where(is_low, given, 0)
@@ -475,7 +483,7 @@
             cols = pl.ds(pl.multiple_of(i * WIDE, WIDE), WIDE)
             gt_ref[...] += dot(w[...], ca_ref[:, :, cols].reshape(BLOCK, WIDE), NT)
 
-        over_weight(project)
+        over_weight(project, 0, w_hbm.shape[1] // WIDE)
         w_copy(0).start()
         w_copy(1).start()
         for i in range(GROUP):
@@ -516,14 +524,18 @@
     lax.fori_loop(0, 10, forward_group, 0)
 
     def finish_forward(i, carry):
-        rows = pl.ds(pl.multiple_of(i * 512, 512), 512)
+        rows = pl.ds(pl.multiple_of((i + 4) % 6 * 512, 512), 512)
         l = l_row[:, rows]
         attn_ref[rows, :] = jnp.transpose(acc_ref[:, rows] / l).astype(BF)
         m_row[:, rows] = m_row[:, rows] * unit + jnp.log2(l)
+
+        @pl.when(i == 1)
+        def _():
+            attn_home.start()
+
         return carry
 
     lax.fori_loop(0, WORK // 512, finish_forward, 0)
-    attn_home.start()
     gs.wait_recv()
 
     def prepare(i, carry):
@@ -609,7 +621,7 @@
         def _():
             near(0, 1, 0)
             relay(0, 1, 0)
-            output_projection()
+            output_projection(0)
 
         @pl.when(s == 3)
         def _():
@@ -620,15 +632,17 @@
         def _():
             near(0, 1, 1)
             relay(0, 1, 1)
-            output_core()
+            output_core(0)
 
         @pl.when(s == 5)
         def _():
             near(1, 1, 1)
             relay(1, 1, 1)
+            output_projection(1)
 
         @pl.when(s == 6)
         def _():
+            output_core(1)
             arrived(0, 1)
             total_first(0, range(4))
             far(0, 2)
@@ -655,7 +669,7 @@
     def _():
         mail.go("y")
 
-    mail.got("row")
+    mail.got(("row", 0), ("row", 1))
     o_ref[...] = (osum[up].astype(F32) + orow[...].astype(F32)).astype(BF)
     dq_home.wait_recv()
 
@@ -672,7 +686,7 @@
         hand.wait_send()
 
 
-COPIES = 1 + 3 + 2 * 20 + 2 * 2 * 6 + 1 + 3
+COPIES = 1 + 3 + 2 * 20 + 2 * 2 * 6 + 1 + 6
 
 
 def layer(unit, scale, k, v, cot, q, w):

time: 134 us -> 132 us (0.985)
  Pallas kernels: 133 us -> 131 us
    pallas_call x1, Pallas kernels: 131 us -> 129 us  [layer(): pl.pallas_call(functools.partial(layer_kernel, unit, scale), out_shape=(j...]
where the time goes in v6:
time: 132 us
  Pallas kernels  131 us (99%)
    pallas_call x1, Pallas kernels, layer(): pl.pallas_call(functools.partial(layer_kernel, unit, scale), out_shape=(j...  129 us

profile of v6, /device:TPU:0, one launch (start us, length us, event | category | flops | bytes accessed | tf_op | source)
XLA Modules:
  0.0 131.6 jit_solution(13517130819694268128)
XLA Ops:
  0.6 128.6 %layer.1 = (bf16[2048,128]{1,0:T(8,128)(2,1)}, bf16[256,128]{1,0:T(8,128)(2,1)}, bf16[256,128]{1,0:T(8,128)(2,1)}, bf16[64,5120]{1,0:T(8,128)(2,1)}) custom-call(bf16[256,128]{1,0:T(8,128)(2,1)} %bitcast.7, bf16[256,128]{1,0:T(8,128)(2,1)} %bitcast.8, bf16[64,5120]{1,0:T(8,128)(2,1)} %cot_ref.1, bf16[2048,128]{1,0:T(8,128)(2,1)} %bitcast.6, ...), custom_call_target="tpu_custom_call" | custom-call | tf_op jit(solution)/shard_map/layer/pallas_call | solution.py:695
  129.2 2.4 %results.1 = (bf16[2048,128]{1,0:T(8,128)(2,1)}, bf16[256,128]{1,0:T(8,128)(2,1)}, bf16[256,128]{1,0:T(8,128)(2,1)}, bf16[64,5120]{1,0:T(8,128)(2,1)}) custom-call(bf16[2048,128]{1,0:T(8,128)(2,1)} %get-tuple-element.12.refs_0_, bf16[256,128]{1,0:T(8,128)(2,1)} %get-tuple-element.13.refs_1_, bf16[256,128]{1,0:T(8,128)(2,1)} %get-tuple-element.14.refs_2_, ...), custom_call_target="tpu_custom_call" | custom-call | tf_op jit(solution)/shard_map/results/pallas_call | solution.py:758

commit v7 on v6

--- a/solution.py
+++ b/solution.py
@@ -265,16 +265,18 @@
         for d in range(2):
             mail.got((n, stage, "near", d), (n, stage, "sum", d))
 
-    def total_first(n, places):
+    def total_first(n):
         at = (x, z)[n]
-        for place_now in places:
-            j = turned((z, x)[n], place_now)
+        for j in range(4):
             for kv in range(2):
                 m_ref[n, j, kv] = (
                     p_ref[n, at, kv, j].astype(F32)
                     + r_ref[n, 0, kv, j].astype(F32)
                     + r_ref[n, 1, kv, j].astype(F32)
                 ).astype(BF)
+        far(n, 2)
+        near(n, 2, 0)
+        near(n, 2, 1)
 
     def total_second(n):
         arrived(n, 2)
@@ -401,7 +403,8 @@
         qpos = ahead + lax.broadcasted_iota(jnp.int32, (keys, n), 1) // GROUP
         return lax.broadcasted_iota(jnp.int32, (keys, n), 0) <= qpos
 
-    def forward_group(s, carry):
+    def forward_group(step, carry):
+        s = jnp.where(step < 6, step, jnp.where(step < 8, step + 2, step - 2))
         n = (1 - y + s) % 2
         i = s % 8 // 2
         off = jnp.where(i == 0, 0, jnp.where(i == 1, 3, jnp.where(i == 2, 1, 2)))
@@ -428,8 +431,8 @@
             mail.go("cot relay")
 
         def arrived_last(n):
-            for step in range(4):
-                mail.got((n, "last", step, 0), (n, "last", step, 1))
+            for i in range(4):
+                mail.got((n, "last", i, 0), (n, "last", i, 1))
 
         @pl.when(s == 6)
         def _():
@@ -588,8 +591,6 @@
                     far_rows = pl.ds(OWN * UNIT, GIVE * UNIT)
                     dq_par[...] = (dqs_ref[far_rows, :] * scale).astype(BF)
                     dq_home.start()
-                    relay(0, 2, 0)
-                    relay(0, 2, 1)
 
             over_pair(n, at, jp, tile, False, between)
             for i in range(2):
@@ -600,10 +601,8 @@
 
             @pl.when(jnp.logical_and(s == 7, jp == 0))
             def _():
-                arrived(1, 1)
-                total_first(1, (0, 1))
-                far(1, 2)
-                near(1, 2, 0)
+                arrived(0, 1)
+                total_first(0)
 
             return carry
 
@@ -643,17 +642,14 @@
         @pl.when(s == 6)
         def _():
             output_core(1)
-            arrived(0, 1)
-            total_first(0, range(4))
-            far(0, 2)
-            near(0, 2, 0)
-            near(0, 2, 1)
 
         return carry
 
     lax.fori_loop(0, 8, backward_group, 0)
-    total_first(1, (2, 3))
-    near(1, 2, 1)
+    arrived(1, 1)
+    total_first(1)
+    relay(0, 2, 0)
+    relay(0, 2, 1)
     dq_ref[...] = (dqs_ref[pl.ds(0, OWN * UNIT), :] * scale).astype(BF)
     relay(1, 2, 0)
     relay(1, 2, 1)

time: 132 us -> 134 us (1.015)
  the two profiles are of different devices: /device:TPU:0 before, /device:TPU:98 now
where the time goes in v7:
time: 134 us
  Pallas kernels  133 us (99%)
    pallas_call x1, Pallas kernels, layer(): pl.pallas_call(functools.partial(layer_kernel, unit, scale), out_shape=(j...  131 us

profile of v7, /device:TPU:98, one launch (start us, length us, event | category | flops | bytes accessed | tf_op | source)
XLA Modules:
  0.0 134.1 jit_solution(5232943629402927744)
XLA Ops:
  0.6 131.0 %layer.1 = (bf16[2048,128]{1,0:T(8,128)(2,1)}, bf16[256,128]{1,0:T(8,128)(2,1)}, bf16[256,128]{1,0:T(8,128)(2,1)}, bf16[64,5120]{1,0:T(8,128)(2,1)}) custom-call(bf16[256,128]{1,0:T(8,128)(2,1)} %bitcast.7, bf16[256,128]{1,0:T(8,128)(2,1)} %bitcast.8, bf16[64,5120]{1,0:T(8,128)(2,1)} %cot_ref.1, bf16[2048,128]{1,0:T(8,128)(2,1)} %bitcast.6, ...), custom_call_target="tpu_custom_call" | custom-call | tf_op jit(solution)/shard_map/layer/pallas_call | solution.py:691
  131.7 2.4 %results.1 = (bf16[2048,128]{1,0:T(8,128)(2,1)}, bf16[256,128]{1,0:T(8,128)(2,1)}, bf16[256,128]{1,0:T(8,128)(2,1)}, bf16[64,5120]{1,0:T(8,128)(2,1)}) custom-call(bf16[2048,128]{1,0:T(8,128)(2,1)} %get-tuple-element.12.refs_0_, bf16[256,128]{1,0:T(8,128)(2,1)} %get-tuple-element.13.refs_1_, bf16[256,128]{1,0:T(8,128)(2,1)} %get-tuple-element.14.refs_2_, ...), custom_call_target="tpu_custom_call" | custom-call | tf_op jit(solution)/shard_map/results/pallas_call | solution.py:754

commit v8 on v6

--- a/solution.py
+++ b/solution.py
@@ -547,8 +547,15 @@
 
     lax.fori_loop(0, WORK // 512, prepare, 0)
 
+    def pass_of(foreign, act):
+        for n in range(2):
+
+            @pl.when(y == (n if foreign else 1 - n))
+            def _():
+                act(n)
+
     def backward_group(s, carry):
-        n = s % 2
+        n = (y + s) % 2
         i = s // 2
         off = jnp.where(i == 0, 2, jnp.where(i == 1, 1, jnp.where(i == 2, 3, 0)))
         at = (jnp.where(n == 0, x, z) + off) % 4
@@ -588,8 +595,7 @@
                     far_rows = pl.ds(OWN * UNIT, GIVE * UNIT)
                     dq_par[...] = (dqs_ref[far_rows, :] * scale).astype(BF)
                     dq_home.start()
-                    relay(0, 2, 0)
-                    relay(0, 2, 1)
+                    pass_of(True, lambda n: (relay(n, 2, 0), relay(n, 2, 1)))
 
             over_pair(n, at, jp, tile, False, between)
             for i in range(2):
@@ -600,75 +606,70 @@
 
             @pl.when(jnp.logical_and(s == 7, jp == 0))
             def _():
-                arrived(1, 1)
-                total_first(1, (0, 1))
-                far(1, 2)
-                near(1, 2, 0)
+                def act(n):
+                    arrived(n, 1)
+                    total_first(n, (0, 1))
+                    far(n, 2)
+                    near(n, 2, 0)
+
+                pass_of(False, act)
 
             return carry
 
         lax.fori_loop(0, 2, pair, 0)
 
+        def hand_on(foreign, d):
+            pass_of(foreign, lambda n: (near(n, 1, d), relay(n, 1, d)))
+
         @pl.when(s == 0)
         def _():
-            far(0, 1)
+            pass_of(True, lambda n: far(n, 1))
 
         @pl.when(s == 1)
         def _():
-            far(1, 1)
+            pass_of(False, lambda n: far(n, 1))
 
         @pl.when(s == 2)
         def _():
-            near(0, 1, 0)
-            relay(0, 1, 0)
+            hand_on(True, 0)
             output_projection(0)
 
         @pl.when(s == 3)
         def _():
-            near(1, 1, 0)
-            relay(1, 1, 0)
+            hand_on(False, 0)
 
         @pl.when(s == 4)
         def _():
-            near(0, 1, 1)
-            relay(0, 1, 1)
+            hand_on(True, 1)
             output_core(0)
 
         @pl.when(s == 5)
         def _():
-            near(1, 1, 1)
-            relay(1, 1, 1)
+            hand_on(False, 1)
             output_projection(1)
 
         @pl.when(s == 6)
         def _():
             output_core(1)
-            arrived(0, 1)
-            total_first(0, range(4))
-            far(0, 2)
-            near(0, 2, 0)
-            near(0, 2, 1)
+
+            def act(n):
+                arrived(n, 1)
+                total_first(n, range(4))
+                far(n, 2)
+                near(n, 2, 0)
+                near(n, 2, 1)
+
+            pass_of(True, act)
 
         return carry
 
     lax.fori_loop(0, 8, backward_group, 0)
-    total_first(1, (2, 3))
-    near(1, 2, 1)
+    pass_of(False, lambda n: (total_first(n, (2, 3)), near(n, 2, 1)))
+    pass_of(True, total_second)
+    mail.go("y")
+    pass_of(False, lambda n: (relay(n, 2, 0), relay(n, 2, 1)))
     dq_ref[...] = (dqs_ref[pl.ds(0, OWN * UNIT), :] * scale).astype(BF)
-    relay(1, 2, 0)
-    relay(1, 2, 1)
-    total_second(0)
-
-    @pl.when(y == 0)
-    def _():
-        mail.go("y")
-
-    total_second(1)
-
-    @pl.when(y == 1)
-    def _():
-        mail.go("y")
-
+    pass_of(False, total_second)
     mail.got(("row", 0), ("row", 1))
     o_ref[...] = (osum[up].astype(F32) + orow[...].astype(F32)).astype(BF)
     dq_home.wait_recv()

time: 132 us -> 129 us (0.977); the launches traced: 132 us -> 127 us
  Pallas kernels: 131 us -> 127 us
    pallas_call x1, Pallas kernels: 129 us -> 124 us  [layer(): pl.pallas_call(functools.partial(layer_kernel, unit, scale), out_shape=(j...]
where the time goes in v8:
time: 129 us; the launch traced here: 127 us
  Pallas kernels  127 us (98%)
    pallas_call x1, Pallas kernels, layer(): pl.pallas_call(functools.partial(layer_kernel, unit, scale), out_shape=(j...  124 us

profile of v8, /device:TPU:0, one launch (start us, length us, event | category | flops | bytes accessed | tf_op | source)
XLA Modules:
  0.0 127.2 jit_solution(15576940600053486802)
XLA Ops:
  0.6 124.2 %layer.1 = (bf16[2048,128]{1,0:T(8,128)(2,1)}, bf16[256,128]{1,0:T(8,128)(2,1)}, bf16[256,128]{1,0:T(8,128)(2,1)}, bf16[64,5120]{1,0:T(8,128)(2,1)}) custom-call(bf16[256,128]{1,0:T(8,128)(2,1)} %bitcast.7, bf16[256,128]{1,0:T(8,128)(2,1)} %bitcast.8, bf16[64,5120]{1,0:T(8,128)(2,1)} %cot_ref.1, bf16[2048,128]{1,0:T(8,128)(2,1)} %bitcast.6, ...), custom_call_target="tpu_custom_call" | custom-call | tf_op jit(solution)/shard_map/layer/pallas_call | solution.py:696
  124.9 2.4 %results.1 = (bf16[2048,128]{1,0:T(8,128)(2,1)}, bf16[256,128]{1,0:T(8,128)(2,1)}, bf16[256,128]{1,0:T(8,128)(2,1)}, bf16[64,5120]{1,0:T(8,128)(2,1)}) custom-call(bf16[2048,128]{1,0:T(8,128)(2,1)} %get-tuple-element.12.refs_0_, bf16[256,128]{1,0:T(8,128)(2,1)} %get-tuple-element.13.refs_1_, bf16[256,128]{1,0:T(8,128)(2,1)} %get-tuple-element.14.refs_2_, ...), custom_call_target="tpu_custom_call" | custom-call | tf_op jit(solution)/shard_map/results/pallas_call | solution.py:759

commit v9 on v8

--- a/solution.py
+++ b/solution.py
@@ -580,31 +580,35 @@
                 axis=0,
             )
             ds = (p * (dot(values, ga, NT) - l_row[:, rows])).astype(BF)
-            ks = pl.ds(pl.multiple_of(j % 2 * BLOCK, BLOCK), blocks * BLOCK)
+            ks = pl.ds(pl.multiple_of(j * BLOCK, BLOCK), blocks * BLOCK)
             dv_ref[ks, :] += dot(p.astype(BF), ga, NN)
             dk_ref[ks, :] += dot(ds, q, NN)
             dqs_ref[rows, :] += dot(ds, keys, TN)
 
-        def pair(jp, carry):
-            dk_ref[...] = jnp.zeros_like(dk_ref)
-            dv_ref[...] = jnp.zeros_like(dv_ref)
-
-            def between():
-                @pl.when(jnp.logical_and(s == 7, jp == 1))
-                def _():
-                    far_rows = pl.ds(OWN * UNIT, GIVE * UNIT)
-                    dq_par[...] = (dqs_ref[far_rows, :] * scale).astype(BF)
-                    dq_home.start()
-                    pass_of(True, lambda n: (relay(n, 2, 0), relay(n, 2, 1)))
-
-            over_pair(n, at, jp, tile, False, between)
-            for i in range(2):
-                ks = pl.ds(i * BLOCK, BLOCK)
-                j = inner(n, 2 * jp + i)
-                p_ref[n, at, 0, j] = (dk_ref[ks, :] * scale).astype(BF)
-                p_ref[n, at, 1, j] = dv_ref[ks, :].astype(BF)
-
-            @pl.when(jnp.logical_and(s == 7, jp == 0))
+        dk_ref[...] = jnp.zeros_like(dk_ref)
+        dv_ref[...] = jnp.zeros_like(dv_ref)
+
+        def quarter(i, carry):
+            ends = s == 7
+            jp = jnp.where(ends, i % 2, i // 2)
+            turn = jnp.where(ends, i // 2, i % 2)
+            over_pair(n, at, jp, tile, False, lambda: None, (turn, turn + 1))
+
+            @pl.when(turn == 1)
+            def _():
+                for k in range(2):
+                    ks = pl.ds(pl.multiple_of((2 * jp + k) * BLOCK, BLOCK), BLOCK)
+                    j = inner(n, 2 * jp + k)
+                    p_ref[n, at, 0, j] = (dk_ref[ks, :] * scale).astype(BF)
+                    p_ref[n, at, 1, j] = dv_ref[ks, :].astype(BF)
+
+            @pl.when(jnp.logical_and(ends, i == 1))
+            def _():
+                far_rows = pl.ds(OWN * UNIT, GIVE * UNIT)
+                dq_par[...] = (dqs_ref[far_rows, :] * scale).astype(BF)
+                dq_home.start()
+
+            @pl.when(jnp.logical_and(ends, i == 2))
             def _():
                 def act(n):
                     arrived(n, 1)
@@ -613,10 +617,11 @@
                     near(n, 2, 0)
 
                 pass_of(False, act)
+                pass_of(True, lambda n: (relay(n, 2, 0), relay(n, 2, 1)))
 
             return carry
 
-        lax.fori_loop(0, 2, pair, 0)
+        lax.fori_loop(0, 4, quarter, 0)
 
         def hand_on(foreign, d):
             pass_of(foreign, lambda n: (near(n, 1, d), relay(n, 1, d)))
@@ -726,8 +731,8 @@
             vm((2,) + part, BF),
             vm(part, BF),
             vm((WORK, HEAD), F32),
-            vm((2 * BLOCK, HEAD), F32),
-            vm((2 * BLOCK, HEAD), F32),
+            vm((4 * BLOCK, HEAD), F32),
+            vm((4 * BLOCK, HEAD), F32),
             vm((2, 4, 2, 4, BLOCK, HEAD), BF),
             vm((2, 2, 4, BLOCK, HEAD), BF),
             vm((2, 2, 2, 4, BLOCK, HEAD), BF),

time: 129 us -> 130 us (level)
  no operation moved by 1% of the time
where the time goes in v9:
time: 130 us; the launch traced here: 127 us
  Pallas kernels  127 us (98%)
    pallas_call x1, Pallas kernels, layer(): pl.pallas_call(functools.partial(layer_kernel, unit, scale), out_shape=(j...  124 us

profile of v9, /device:TPU:0, one launch (start us, length us, event | category | flops | bytes accessed | tf_op | source)
XLA Modules:
  0.0 127.2 jit_solution(6410465097866395578)
XLA Ops:
  0.6 124.2 %layer.1 = (bf16[2048,128]{1,0:T(8,128)(2,1)}, bf16[256,128]{1,0:T(8,128)(2,1)}, bf16[256,128]{1,0:T(8,128)(2,1)}, bf16[64,5120]{1,0:T(8,128)(2,1)}) custom-call(bf16[256,128]{1,0:T(8,128)(2,1)} %bitcast.7, bf16[256,128]{1,0:T(8,128)(2,1)} %bitcast.8, bf16[64,5120]{1,0:T(8,128)(2,1)} %cot_ref.1, bf16[2048,128]{1,0:T(8,128)(2,1)} %bitcast.6, ...), custom_call_target="tpu_custom_call" | custom-call | tf_op jit(solution)/shard_map/layer/pallas_call | solution.py:701
  124.8 2.4 %results.1 = (bf16[2048,128]{1,0:T(8,128)(2,1)}, bf16[256,128]{1,0:T(8,128)(2,1)}, bf16[256,128]{1,0:T(8,128)(2,1)}, bf16[64,5120]{1,0:T(8,128)(2,1)}) custom-call(bf16[2048,128]{1,0:T(8,128)(2,1)} %get-tuple-element.12.refs_0_, bf16[256,128]{1,0:T(8,128)(2,1)} %get-tuple-element.13.refs_1_, bf16[256,128]{1,0:T(8,128)(2,1)} %get-tuple-element.14.refs_2_, ...), custom_call_target="tpu_custom_call" | custom-call | tf_op jit(solution)/shard_map/results/pallas_call | solution.py:764

commit v10 on v8

--- a/solution.py
+++ b/solution.py
@@ -401,7 +401,8 @@
         qpos = ahead + lax.broadcasted_iota(jnp.int32, (keys, n), 1) // GROUP
         return lax.broadcasted_iota(jnp.int32, (keys, n), 0) <= qpos
 
-    def forward_group(s, carry):
+    def forward_group(step, carry):
+        s = jnp.where(step < 6, step, jnp.where(step < 8, step + 2, step - 2))
         n = (1 - y + s) % 2
         i = s % 8 // 2
         off = jnp.where(i == 0, 0, jnp.where(i == 1, 3, jnp.where(i == 2, 1, 2)))
@@ -428,8 +429,8 @@
             mail.go("cot relay")
 
         def arrived_last(n):
-            for step in range(4):
-                mail.got((n, "last", step, 0), (n, "last", step, 1))
+            for i in range(4):
+                mail.got((n, "last", i, 0), (n, "last", i, 1))
 
         @pl.when(s == 6)
         def _():

time: 129 us -> 129 us (level)
  the two profiles are of different devices: /device:TPU:0 before, /device:TPU:16 now
where the time goes in v10:
time: 129 us
  Pallas kernels  128 us (99%)
    pallas_call x1, Pallas kernels, layer(): pl.pallas_call(functools.partial(layer_kernel, unit, scale), out_shape=(j...  126 us

profile of v10, /device:TPU:16, one launch (start us, length us, event | category | flops | bytes accessed | tf_op | source)
XLA Modules:
  0.0 128.6 jit_solution(9971716298698406033)
XLA Ops:
  0.6 125.6 %layer.1 = (bf16[2048,128]{1,0:T(8,128)(2,1)}, bf16[256,128]{1,0:T(8,128)(2,1)}, bf16[256,128]{1,0:T(8,128)(2,1)}, bf16[64,5120]{1,0:T(8,128)(2,1)}) custom-call(bf16[256,128]{1,0:T(8,128)(2,1)} %bitcast.7, bf16[256,128]{1,0:T(8,128)(2,1)} %bitcast.8, bf16[64,5120]{1,0:T(8,128)(2,1)} %cot_ref.1, bf16[2048,128]{1,0:T(8,128)(2,1)} %bitcast.6, ...), custom_call_target="tpu_custom_call" | custom-call | tf_op jit(solution)/shard_map/layer/pallas_call | solution.py:697
  126.2 2.4 %results.1 = (bf16[2048,128]{1,0:T(8,128)(2,1)}, bf16[256,128]{1,0:T(8,128)(2,1)}, bf16[256,128]{1,0:T(8,128)(2,1)}, bf16[64,5120]{1,0:T(8,128)(2,1)}) custom-call(bf16[2048,128]{1,0:T(8,128)(2,1)} %get-tuple-element.12.refs_0_, bf16[256,128]{1,0:T(8,128)(2,1)} %get-tuple-element.13.refs_1_, bf16[256,128]{1,0:T(8,128)(2,1)} %get-tuple-element.14.refs_2_, ...), custom_call_target="tpu_custom_call" | custom-call | tf_op jit(solution)/shard_map/results/pallas_call | solution.py:760
